TPU v7x, 256 devices: a whole 4x4x8 slice. The times are simulated.
256 devices in a mesh: seg: 8 (over y, core), sec: 32 (over z, x).
Axes of the slice: x: 4, y: 4, z: 8, core: 2. Of those that a mesh axis runs over, the one named last changes fastest.
Arguments:
- state_blocks: bfloat16 [8, 64, 256, 256], P('seg', 'sec')
- gauge_offset: float32 [8, 64, 256, 256], P('seg', 'sec'), may hold values from -0.1125 to 0.1125
- left_env: bfloat16 [8, 64, 16, 256, 256], P('seg', 'sec'), may hold values from -0.09375 to 0.09375
- right_env: bfloat16 [8, 64, 16, 256, 256], P('seg', 'sec'), may hold values from -0.375 to 0.375
- mpo_mask: int32 [64, 16], P('sec'), may hold values 0 or 1
- charge: int32 [16], replicated, may hold values from -1 to 1, as said below
- block_dims: int32 [64], P('sec'), may hold values from 64 to 256, as said below
Outputs:
- krylov: bfloat16 [8, 64, 256, 256], P('seg', 'sec')
- env_next: bfloat16 [8, 64, 16, 256, 256], P('seg', 'sec')
- rayleigh: float32 [8], P('seg')
Inputs may be any that keep to these rules, and one draw needn't show every extreme that they name: `charge`: exactly 4 channels carry +1 and exactly 4 carry -1, the others 0. `block_dims`: some sector has exactly 256 live rows in every draw.
All inputs are finite; a program needn't handle non-finite values. No bound on the sum of `mpo_mask` on one device may be relied on, other than what follows from the above.
Results may differ from a plain program's by a relative error of at most 0.018.
Values may be sent and summed in bfloat16 or wider, within the bound.
No kernel may reach another device: no remote copies, remote signals or barrier semaphores. Data moves between devices by JAX's collectives and lax.ppermute only.
A program may use at most 64 MiB of HBM per device.

v0:
```python
import jax
import jax.numpy as jnp
from jax import lax
from jax.sharding import PartitionSpec as P


def extended(cells, sides, width):
    for axis, dim in sides:
        count = lax.axis_size(axis)
        ends = count - 1
        head = lax.slice_in_dim(cells, 0, width, axis=dim)
        tail = lax.slice_in_dim(cells, cells.shape[dim] - width, cells.shape[dim], axis=dim)
        cells = jnp.concatenate(
            [
                lax.ppermute(tail, axis, [(i, (i + 1) % count) for i in range(ends)]),
                cells,
                lax.ppermute(head, axis, [((i + 1) % count, i) for i in range(ends)]),
            ],
            axis=dim,
        )
    return cells


def passed_along(shard, axis, by):
    length = lax.axis_size(axis)
    pairs = [(i, i + by) for i in range(length) if 0 <= i + by < length]
    return lax.ppermute(shard, axis, pairs)


def matmul_high(first, second):
    return jnp.einsum("sij,sjk->sik", first, second, precision=lax.Precision.HIGHEST)


def pick_channels(below, above, middle, charge):
    upward = (charge == 1)[None, :, None, None]
    downward = (charge == -1)[None, :, None, None]
    return jnp.where(upward, below, jnp.where(downward, above, middle))


def hamiltonian(field, left_here, right_here, mpo_mask, charge, cell_mask):
    padded = extended(field, (("sec", 0),), 1)
    select = pick_channels(padded[:-2][:, None], padded[2:][:, None], field[:, None], charge)
    partial_value = jnp.einsum(
        "swij,swjk->swik", left_here, select, preferred_element_type=jnp.float32
    ).astype(jnp.bfloat16)
    partial_value = partial_value * mpo_mask[:, :, None, None].astype(jnp.bfloat16)
    image = jnp.einsum(
        "swij,swjk->sik", partial_value, right_here, preferred_element_type=jnp.float32
    )
    return (image * cell_mask).astype(jnp.bfloat16)


def local(state_blocks, gauge_offset, left_env, right_env, mpo_mask, charge, block_dims):
    sectors_here = state_blocks.shape[1]
    width = state_blocks.shape[-1]
    sector_total = sectors_here * lax.axis_size("sec")
    identity_blocks = jnp.broadcast_to(
        jnp.eye(width, dtype=jnp.float32), (sectors_here, width, width)
    )
    gauge = gauge_offset[0] + identity_blocks
    position = lax.axis_index("seg")
    current = identity_blocks
    for section in range(lax.axis_size("seg") - 1):
        outgoing = matmul_high(gauge, current)
        incoming = passed_along(outgoing, "seg", 1)
        current = jnp.where(position == section + 1, incoming, current)
    inclusive = matmul_high(gauge, current)
    live_rows = jnp.arange(width)[None, :] < block_dims[:, None]
    cell_mask = (live_rows[:, :, None] & live_rows[:, None, :]).astype(jnp.float32)
    left_here = left_env[0]
    right_here = right_env[0]
    x = (matmul_high(inclusive, state_blocks[0].astype(jnp.float32)) * cell_mask).astype(
        jnp.bfloat16
    )
    first = hamiltonian(x, left_here, right_here, mpo_mask, charge, cell_mask)
    x_wide = x.astype(jnp.float32)
    first_wide = first.astype(jnp.float32)
    norm_state, correlation = lax.psum(
        (jnp.sum(x_wide * x_wide), jnp.sum(x_wide * first_wide)), "sec"
    )
    rayleigh = correlation / norm_state
    residue = first_wide - rayleigh * x_wide
    residue_norm = lax.psum(jnp.sum(residue * residue), "sec")
    residue_scale = jnp.sqrt(residue_norm / (sector_total * width * width) + 1e-06)
    lanczos_vec = (residue / residue_scale).astype(jnp.bfloat16)
    krylov = hamiltonian(lanczos_vec, left_here, right_here, mpo_mask, charge, cell_mask)
    left_x = jnp.einsum("swij,sjk->swik", left_here, x, preferred_element_type=jnp.float32).astype(
        jnp.bfloat16
    )
    contrib = jnp.einsum("sia,swij->swaj", x, left_x, preferred_element_type=jnp.float32).astype(
        jnp.bfloat16
    )
    padded = extended(contrib, (("sec", 0),), 1)
    below = padded[:-2]
    above = padded[2:]
    env_next = pick_channels(below, above, contrib, charge)
    return (krylov[None], env_next[None], jnp.reshape(rayleigh, (1,)))


def solution(mesh):
    return jax.shard_map(
        local,
        mesh=mesh,
        in_specs=(
            P("seg", "sec", None, None),
            P("seg", "sec", None, None),
            P("seg", "sec", None, None, None),
            P("seg", "sec", None, None, None),
            P("sec", None),
            P(),
            P("sec"),
        ),
        out_specs=(P("seg", "sec", None, None), P("seg", "sec", None, None, None), P("seg")),
        check_vma=False,
    )
```

profile of v0, /device:TPU:110, one launch (start us, length us, event | category | flops | bytes accessed | tf_op | source)
XLA Modules:
  0.0 333.5 jit_solution(16190422436957318555)
XLA Ops:
  0.6 0.0 copy-start
  0.6 0.0 copy-start.1
  0.7 1.8 fusion.149
  2.4 1.9 collective-permute-start
  4.4 8.6 %collective-permute-done = f32[2,256,256]{2,1,0:T(8,128)S(1)} collective-permute-done((f32[2,256,256]{2,1,0:T(8,128)S(1)}, f32[2,256,256]{2,1,0:T(8,128)S(1)}, u32[]{:S(2)}, u32[]{:S(2)}) %collective-permute-start) | collective-permute-done | bytes 524320 | tf_op jit(solution)/shard_map/ppermute | solution.py:27
  12.9 1.7 fusion.142
  14.7 1.9 collective-permute-start.1
  16.6 8.6 %collective-permute-done.1 = f32[2,256,256]{2,1,0:T(8,128)S(1)} collective-permute-done((f32[2,256,256]{2,1,0:T(8,128)S(1)}, f32[2,256,256]{2,1,0:T(8,128)S(1)}, u32[]{:S(2)}, u32[]{:S(2)}) %collective-permute-start.1) | collective-permute-done | bytes 524320 | tf_op jit(solution)/shard_map/ppermute | solution.py:27
  25.2 0.0 copy-done.1
  25.2 0.7 fusion.148
  25.9 1.9 collective-permute-start.2
  27.8 8.6 %collective-permute-done.2 = f32[2,256,256]{2,1,0:T(8,128)S(1)} collective-permute-done((f32[2,256,256]{2,1,0:T(8,128)S(1)}, f32[2,256,256]{2,1,0:T(8,128)S(1)}, u32[]{:S(2)}, u32[]{:S(2)}) %collective-permute-start.2) | collective-permute-done | bytes 524320 | tf_op jit(solution)/shard_map/ppermute | solution.py:27
  36.4 0.1 broadcast_select_fusion
  36.5 0.7 fusion.147
  37.2 1.9 collective-permute-start.3
  39.1 0.0 copy-start.2
  39.1 0.0 copy-start.3
  39.2 0.0 copy-start.4
  39.2 8.5 %collective-permute-done.3 = f32[2,256,256]{2,1,0:T(8,128)S(1)} collective-permute-done((f32[2,256,256]{2,1,0:T(8,128)S(1)}, f32[2,256,256]{2,1,0:T(8,128)S(1)}, u32[]{:S(2)}, u32[]{:S(2)}) %collective-permute-start.3) | collective-permute-done | bytes 524320 | tf_op jit(solution)/shard_map/ppermute | solution.py:27
  47.7 0.7 fusion.146
  48.4 1.9 collective-permute-start.4
  50.3 8.6 %collective-permute-done.4 = f32[2,256,256]{2,1,0:T(8,128)S(1)} collective-permute-done((f32[2,256,256]{2,1,0:T(8,128)S(1)}, f32[2,256,256]{2,1,0:T(8,128)S(1)}, u32[]{:S(2)}, u32[]{:S(2)}) %collective-permute-start.4) | collective-permute-done | bytes 524320 | tf_op jit(solution)/shard_map/ppermute | solution.py:27
  58.9 0.1 broadcast_select_fusion.2
  59.0 0.7 fusion.145
  59.7 1.9 collective-permute-start.5
  61.6 8.6 %collective-permute-done.5 = f32[2,256,256]{2,1,0:T(8,128)S(1)} collective-permute-done((f32[2,256,256]{2,1,0:T(8,128)S(1)}, f32[2,256,256]{2,1,0:T(8,128)S(1)}, u32[]{:S(2)}, u32[]{:S(2)}) %collective-permute-start.5) | collective-permute-done | bytes 524320 | tf_op jit(solution)/shard_map/ppermute | solution.py:27
  70.2 0.7 fusion.144
  70.9 1.9 collective-permute-start.6
  72.8 0.0 copy-done.2
  72.8 0.1 iota_compare_fusion.1
  72.9 0.0 copy-done.4
  72.9 8.5 %collective-permute-done.6 = f32[2,256,256]{2,1,0:T(8,128)S(1)} collective-permute-done((f32[2,256,256]{2,1,0:T(8,128)S(1)}, f32[2,256,256]{2,1,0:T(8,128)S(1)}, u32[]{:S(2)}, u32[]{:S(2)}) %collective-permute-start.6) | collective-permute-done | bytes 524320 | tf_op jit(solution)/shard_map/ppermute | solution.py:27
  81.4 0.7 fusion.140
  82.1 0.4 fusion.127
  82.5 4.9 %collective-permute-start.7 = (bf16[1,256,256]{2,1,0:T(8,128)(2,1)S(1)}, bf16[1,256,256]{2,1,0:T(8,128)(2,1)S(1)}, u32[]{:S(2)}, u32[]{:S(2)}) collective-permute-start(bf16[1,256,256]{2,1,0:T(8,128)(2,1)S(1)} %get-tuple-element.18), channel_id=1, source_target_pairs={{0,1},{1,2},{2,3},{3,4},{4,5},{5,6},{6,7},{7,8},{8,9},{9,10},{10,1... | collective-permute-start | bytes 393224 | tf_op jit(solution)/shard_map/ppermute | solution.py:15
  87.5 1.9 collective-permute-start.8
  89.4 6.6 %convert_bitcast_fusion = bf16[2,16,256,256]{2,3,1,0:T(8,128)(2,1)} fusion(bf16[1,2,16,256,256]{4,3,2,1,0:T(8,128)(2,1)} %param.9, bf16[2,256,256]{2,1,0:T(8,128)(2,1)S(1)} %fusion.127), kind=kOutput, calls=%fused_computation.19 | convolution fusion | flops 2151677952 | bytes 8650752 | tf_op jit(solution)/shard_map/sia,swij->swaj/dot_general | solution.py:90
  96.0 4.6 %fusion.164 = (bf16[1,16,256,256]{2,3,1,0:T(8,128)(2,1)}, bf16[1,16,256,256]{2,3,1,0:T(8,128)(2,1)}) fusion(bf16[2,16,256,256]{2,3,1,0:T(8,128)(2,1)} %convert_bitcast_fusion), kind=kLoop, calls=%fused_computation.96 | loop fusion | bytes 8388608 | tf_op jit(solution)/shard_map/slice | solution.py:12
  100.6 0.1 copy.12
  100.8 7.2 %collective-permute-start.11 = (bf16[1,16,256,256]{2,3,1,0:T(8,128)(2,1)}, bf16[1,16,256,256]{2,3,1,0:T(8,128)(2,1)S(1)}, u32[]{:S(2)}, u32[]{:S(2)}) collective-permute-start(bf16[1,16,256,256]{2,3,1,0:T(8,128)(2,1)} %get-tuple-element.10), channel_id=1, source_target_pairs={{0,1},{1,2},{2,3},{3,4},{4,5},{5,6},{6,7},{7,8},{8,9},{9,10},{10,1... | collective-permute-start | bytes 6291464 | tf_op jit(solution)/shard_map/ppermute | solution.py:15
  108.0 2.1 collective-permute-start.12
  110.1 0.0 collective-permute-done.7
  110.2 0.0 collective-permute-done.8
  110.2 1.0 pad_maximum_fusion.5
  111.1 0.8 copy.10
  112.0 0.8 copy.11
  112.8 6.9 %fusion.138 = (f32[]{:T(128)}, f32[]{:T(128)}, f32[2,256,256]{2,1,0:T(8,128)S(1)}) fusion(bf16[2,256,256]{2,1,0:T(8,128)(2,1)S(1)} %fusion.127, bf16[1,2,16,256,256]{4,3,2,1,0:T(8,128)(2,1)} %param.10, bf16[2,16]{1,0:T(2,128)(2,1)S(1)} %convert_element_type.55, bf16[1,2,16,256,256]{4,3,2,1,0:T(8,128)(2,1)} %param.9, ...), kind=kOutput, calls=%fused_computation.55 | convolution fusion | flops 2157051904 | bytes 9962088 | tf_op jit(solution)/shard_map/swij,swjk->sik/dot_general | solution.py:47
  119.7 101.5 %all-reduce = (f32[]{:T(128)}, f32[]{:T(128)}) all-reduce(f32[]{:T(128)} %get-tuple-element.7, f32[]{:T(128)} %get-tuple-element.6), channel_id=1, replica_groups=mesh['seg'=8,'sec'=32] {'sec'}, use_global_device_ids=true, to_apply=%region_1.2 | all-reduce | flops 2 | bytes 16 | tf_op jit(solution)/shard_map/psum | solution.py:78
  222.5 0.7 multiply_reduce_fusion
  223.3 72.5 %psum.23 = f32[]{:T(128)} all-reduce(f32[]{:T(128)} %multiply_reduce_fusion), channel_id=1, replica_groups=mesh['seg'=8,'sec'=32] {'sec'}, use_global_device_ids=true, to_apply=%region_5.6 | all-reduce | flops 1 | bytes 8 | tf_op jit(solution)/shard_map/psum | solution.py:83
  296.5 0.1 divide_convert_fusion
  296.6 5.3 %collective-permute-start.9 = (bf16[1,256,256]{2,1,0:T(8,128)(2,1)S(1)}, bf16[1,256,256]{2,1,0:T(8,128)(2,1)S(1)}, u32[]{:S(2)}, u32[]{:S(2)}) collective-permute-start(bf16[1,256,256]{2,1,0:T(8,128)(2,1)S(1)} %get-tuple-element.14), channel_id=1, source_target_pairs={{0,1},{1,2},{2,3},{3,4},{4,5},{5,6},{6,7},{7,8},{8,9},{9,10},{10,1... | collective-permute-start | bytes 393224 | tf_op jit(solution)/shard_map/ppermute | solution.py:15
  301.9 1.9 collective-permute-start.10
  303.8 0.1 copy.15
  303.9 0.4 collective-permute-done.9
  304.4 7.8 %collective-permute-done.10 = bf16[1,256,256]{2,1,0:T(8,128)(2,1)} collective-permute-done((bf16[1,256,256]{2,1,0:T(8,128)(2,1)S(1)}, bf16[1,256,256]{2,1,0:T(8,128)(2,1)}, u32[]{:S(2)}, u32[]{:S(2)}) %collective-permute-start.10) | collective-permute-done | bytes 131104 | tf_op jit(solution)/shard_map/ppermute | solution.py:17
  312.2 1.0 pad_maximum_fusion.3
  313.1 0.1 copy.13
  313.3 0.1 copy.14
  313.4 6.7 %fusion.128 = bf16[1,2,256,256]{3,2,1,0:T(8,128)(2,1)} fusion(bf16[1,2,16,256,256]{4,3,2,1,0:T(8,128)(2,1)} %param.10, bf16[1,2,16,256,256]{4,3,2,1,0:T(8,128)(2,1)} %param.9, pred[16]{0:T(512)(128)(4,1)S(1)} %get-tuple-element.21, pred[16]{0:T(512)(128)(4,1)S(1)} %get-tuple-element.20, bf16[2,256,256]{1,2,0:T(8,128)(2,1)S(1)} %copy.15, ...), kind=kOutput, calls=%fused_computation.50 | convolution fusion | flops 2156265472 | bytes 9437792 | tf_op jit(solution)/shard_map/swij,swjk->sik/dot_general | solution.py:47
  320.1 0.0 collective-permute-done.11
  320.1 0.0 collective-permute-done.12
  320.1 6.1 %fusion.2 = bf16[1,2,16,256,256]{3,4,2,1,0:T(8,128)(2,1)} fusion(bf16[2,16,256,256]{2,3,1,0:T(8,128)(2,1)} %convert_bitcast_fusion, bf16[1,16,256,256]{2,3,1,0:T(8,128)(2,1)} %collective-permute-done.12, bf16[1,16,256,256]{2,3,1,0:T(8,128)(2,1)S(1)} %collective-permute-done.11, pred[16]{0:T(512)(128)(4,1)S(1)} %get-tuple-element.21, ...), kind=kLoop, calls=%fused_computation.3 | loop fusion | flops 8388608 | bytes 12582944 | tf_op jit(solution)/shard_map/broadcast_in_dim | solution.py:97
  326.2 6.2 %copy.16 = bf16[1,2,16,256,256]{4,3,2,1,0:T(8,128)(2,1)} copy(bf16[1,2,16,256,256]{3,4,2,1,0:T(8,128)(2,1)} %fusion.2) | data formatting | bytes 8388608
  (7 shorter events, 0.1 us)
Async XLA Ops:
  0.6 81.5 %copy-start = (bf16[1,2,256,256]{3,2,1,0:T(8,128)(2,1)S(1)}, bf16[1,2,256,256]{3,2,1,0:T(8,128)(2,1)}, u32[]{:S(2)}) copy-start(bf16[1,2,256,256]{3,2,1,0:T(8,128)(2,1)} %param.7) | copy-start | bytes 786436
  0.6 24.5 %copy-start.1 = (f32[1,2,256,256]{3,2,1,0:T(8,128)S(1)}, f32[1,2,256,256]{3,2,1,0:T(8,128)}, u32[]{:S(2)}) copy-start(f32[1,2,256,256]{3,2,1,0:T(8,128)} %param.8) | copy-start | bytes 1572868
  2.4 10.5 %collective-permute-start = (f32[2,256,256]{2,1,0:T(8,128)S(1)}, f32[2,256,256]{2,1,0:T(8,128)S(1)}, u32[]{:S(2)}, u32[]{:S(2)}) collective-permute-start(f32[2,256,256]{2,1,0:T(8,128)S(1)} %fusion.149), channel_id=1, source_target_pairs={{0,32},{32,64},{64,96},{96,128},{128,160},{160,192},{192,224},{1,3... | collective-permute-start | bytes 1572872 | tf_op jit(solution)/shard_map/ppermute | solution.py:27
  14.7 10.5 %collective-permute-start.1 = (f32[2,256,256]{2,1,0:T(8,128)S(1)}, f32[2,256,256]{2,1,0:T(8,128)S(1)}, u32[]{:S(2)}, u32[]{:S(2)}) collective-permute-start(f32[2,256,256]{2,1,0:T(8,128)S(1)} %fusion.142), channel_id=1, source_target_pairs={{0,32},{32,64},{64,96},{96,128},{128,160},{160,192},{192,224},{1,3... | collective-permute-start | bytes 1572872 | tf_op jit(solution)/shard_map/ppermute | solution.py:27
  25.9 10.5 %collective-permute-start.2 = (f32[2,256,256]{2,1,0:T(8,128)S(1)}, f32[2,256,256]{2,1,0:T(8,128)S(1)}, u32[]{:S(2)}, u32[]{:S(2)}) collective-permute-start(f32[2,256,256]{2,1,0:T(8,128)S(1)} %fusion.148), channel_id=1, source_target_pairs={{0,32},{32,64},{64,96},{96,128},{128,160},{160,192},{192,224},{1,3... | collective-permute-start | bytes 1572872 | tf_op jit(solution)/shard_map/ppermute | solution.py:27
  37.2 10.5 %collective-permute-start.3 = (f32[2,256,256]{2,1,0:T(8,128)S(1)}, f32[2,256,256]{2,1,0:T(8,128)S(1)}, u32[]{:S(2)}, u32[]{:S(2)}) collective-permute-start(f32[2,256,256]{2,1,0:T(8,128)S(1)} %fusion.147), channel_id=1, source_target_pairs={{0,32},{32,64},{64,96},{96,128},{128,160},{160,192},{192,224},{1,3... | collective-permute-start | bytes 1572872 | tf_op jit(solution)/shard_map/ppermute | solution.py:27
  39.1 33.7 %copy-start.2 = (s32[2,16]{1,0:T(2,128)S(1)}, s32[2,16]{1,0:T(2,128)}, u32[]{:S(2)}) copy-start(s32[2,16]{1,0:T(2,128)} %param.11) | copy-start | bytes 388
  39.1 33.7 %copy-start.3 = (s32[2]{0:T(128)S(1)}, s32[2]{0:T(128)}, u32[]{:S(2)}) copy-start(s32[2]{0:T(128)} %param.13) | copy-start | bytes 28
  39.2 33.8 %copy-start.4 = (s32[16]{0:T(128)S(1)}, s32[16]{0:T(128)}, u32[]{:S(2)}) copy-start(s32[16]{0:T(128)} %param.12) | copy-start | bytes 196
  48.4 10.5 %collective-permute-start.4 = (f32[2,256,256]{2,1,0:T(8,128)S(1)}, f32[2,256,256]{2,1,0:T(8,128)S(1)}, u32[]{:S(2)}, u32[]{:S(2)}) collective-permute-start(f32[2,256,256]{2,1,0:T(8,128)S(1)} %fusion.146), channel_id=1, source_target_pairs={{0,32},{32,64},{64,96},{96,128},{128,160},{160,192},{192,224},{1,3... | collective-permute-start | bytes 1572872 | tf_op jit(solution)/shard_map/ppermute | solution.py:27
  59.7 10.5 %collective-permute-start.5 = (f32[2,256,256]{2,1,0:T(8,128)S(1)}, f32[2,256,256]{2,1,0:T(8,128)S(1)}, u32[]{:S(2)}, u32[]{:S(2)}) collective-permute-start(f32[2,256,256]{2,1,0:T(8,128)S(1)} %fusion.145), channel_id=1, source_target_pairs={{0,32},{32,64},{64,96},{96,128},{128,160},{160,192},{192,224},{1,3... | collective-permute-start | bytes 1572872 | tf_op jit(solution)/shard_map/ppermute | solution.py:27
  70.9 10.5 %collective-permute-start.6 = (f32[2,256,256]{2,1,0:T(8,128)S(1)}, f32[2,256,256]{2,1,0:T(8,128)S(1)}, u32[]{:S(2)}, u32[]{:S(2)}) collective-permute-start(f32[2,256,256]{2,1,0:T(8,128)S(1)} %fusion.144), channel_id=1, source_target_pairs={{0,32},{32,64},{64,96},{96,128},{128,160},{160,192},{192,224},{1,3... | collective-permute-start | bytes 1572872 | tf_op jit(solution)/shard_map/ppermute | solution.py:27
  82.5 27.6 %collective-permute-start.7 = (bf16[1,256,256]{2,1,0:T(8,128)(2,1)S(1)}, bf16[1,256,256]{2,1,0:T(8,128)(2,1)S(1)}, u32[]{:S(2)}, u32[]{:S(2)}) collective-permute-start(bf16[1,256,256]{2,1,0:T(8,128)(2,1)S(1)} %get-tuple-element.18), channel_id=1, source_target_pairs={{0,1},{1,2},{2,3},{3,4},{4,5},{5,6},{6,7},{7,8},{8,9},{9,10},{10,1... | collective-permute-start | bytes 393224 | tf_op jit(solution)/shard_map/ppermute | solution.py:15
  87.5 22.7 %collective-permute-start.8 = (bf16[1,256,256]{2,1,0:T(8,128)(2,1)S(1)}, bf16[1,256,256]{2,1,0:T(8,128)(2,1)}, u32[]{:S(2)}, u32[]{:S(2)}) collective-permute-start(bf16[1,256,256]{2,1,0:T(8,128)(2,1)S(1)} %get-tuple-element.19), channel_id=1, source_target_pairs={{1,0},{2,1},{3,2},{4,3},{5,4},{6,5},{7,6},{8,7},{9,8},{10,9},{11,1... | collective-permute-start | bytes 393224 | tf_op jit(solution)/shard_map/ppermute | solution.py:17
  100.8 219.3 %collective-permute-start.11 = (bf16[1,16,256,256]{2,3,1,0:T(8,128)(2,1)}, bf16[1,16,256,256]{2,3,1,0:T(8,128)(2,1)S(1)}, u32[]{:S(2)}, u32[]{:S(2)}) collective-permute-start(bf16[1,16,256,256]{2,3,1,0:T(8,128)(2,1)} %get-tuple-element.10), channel_id=1, source_target_pairs={{0,1},{1,2},{2,3},{3,4},{4,5},{5,6},{6,7},{7,8},{8,9},{9,10},{10,1... | collective-permute-start | bytes 6291464 | tf_op jit(solution)/shard_map/ppermute | solution.py:15
  108.0 212.1 %collective-permute-start.12 = (bf16[1,16,256,256]{2,3,1,0:T(8,128)(2,1)}, bf16[1,16,256,256]{2,3,1,0:T(8,128)(2,1)}, u32[]{:S(2)}, u32[]{:S(2)}) collective-permute-start(bf16[1,16,256,256]{2,3,1,0:T(8,128)(2,1)} %get-tuple-element.11), channel_id=1, source_target_pairs={{1,0},{2,1},{3,2},{4,3},{5,4},{6,5},{7,6},{8,7},{9,8},{10,9},{11,1... | collective-permute-start | bytes 6291464 | tf_op jit(solution)/shard_map/ppermute | solution.py:17
  296.6 7.8 %collective-permute-start.9 = (bf16[1,256,256]{2,1,0:T(8,128)(2,1)S(1)}, bf16[1,256,256]{2,1,0:T(8,128)(2,1)S(1)}, u32[]{:S(2)}, u32[]{:S(2)}) collective-permute-start(bf16[1,256,256]{2,1,0:T(8,128)(2,1)S(1)} %get-tuple-element.14), channel_id=1, source_target_pairs={{0,1},{1,2},{2,3},{3,4},{4,5},{5,6},{6,7},{7,8},{8,9},{9,10},{10,1... | collective-permute-start | bytes 393224 | tf_op jit(solution)/shard_map/ppermute | solution.py:15
  301.9 10.3 %collective-permute-start.10 = (bf16[1,256,256]{2,1,0:T(8,128)(2,1)S(1)}, bf16[1,256,256]{2,1,0:T(8,128)(2,1)}, u32[]{:S(2)}, u32[]{:S(2)}) collective-permute-start(bf16[1,256,256]{2,1,0:T(8,128)(2,1)S(1)} %get-tuple-element.15), channel_id=1, source_target_pairs={{1,0},{2,1},{3,2},{4,3},{5,4},{6,5},{7,6},{8,7},{9,8},{10,9},{11,1... | collective-permute-start | bytes 393224 | tf_op jit(solution)/shard_map/ppermute | solution.py:17
where the time goes:
time: 334 us
  blocking collectives  174 us (52%)
  waiting for transfers between devices  68 us (20%)
  starting transfers between devices  36.9 us (11%)
  matrix products  28.2 us (8%)
  local copies, waits for them, and re-layouts  13.1 us (4%)
  other arithmetic  9.12 us (3%)
  between operations  4.18 us (1%)
    psum x1, blocking collectives, local(): lax.psum((jnp.sum(x_wide * x_wide), jnp.sum(x_wide * first_wide)), 'sec')  101 us
    psum x1, blocking collectives, local(): residue_norm = lax.psum(jnp.sum(residue * residue), 'sec')  72.5 us
    ppermute x7, waiting for transfers between devices, passed_along(): return lax.ppermute(shard, axis, pairs)  59.8 us
    ppermute x3, starting transfers between devices, extended(): lax.ppermute(tail, axis, [(i, (i + 1) % count) for i in range(ends)])  17.5 us
    dot_general x2, matrix products, hamiltonian(): jnp.einsum('swij,swjk->sik', partial_value, right_here, preferred_element...  13.6 us
    ppermute x7, starting transfers between devices, passed_along(): return lax.ppermute(shard, axis, pairs)  13.4 us
    dot_general x9, matrix products, matmul_high(): jnp.einsum('sij,sjk->sik', first, second, precision=lax.Precision.HIGHEST)  8.02 us
    ppermute x3, waiting for transfers between devices, extended(): lax.ppermute(head, axis, [((i + 1) % count, i) for i in range(ends)])  7.79 us
  transfers between devices with their start and end apart: 13, of which 9 were waited for; matrix products, arithmetic and copies ran while one was open for 9% of the time, Pallas kernels for 0%

commit v1 on v0

v1 whole, which is shorter than its diff:
```python
import functools

import jax
import jax.numpy as jnp
from jax import lax
from jax.experimental import pallas as pl
from jax.experimental.pallas import tpu as pltpu
from jax.sharding import PartitionSpec as P

F32 = jnp.float32
BF16 = jnp.bfloat16
AXES = ("seg", "sec")
QUARTER = 4
MIB = 1 << 20


def dot(first, second):
    return lax.dot_general(
        first, second, (((1,), (0,)), ((), ())), preferred_element_type=F32
    )


def vmem(count):
    return [pl.BlockSpec(memory_space=pltpu.VMEM)] * count


def smem(count):
    return [pl.BlockSpec(memory_space=pltpu.SMEM)] * count


def anywhere(count):
    return [pl.BlockSpec(memory_space=pl.ANY)] * count


def cost(products, size, bytes_accessed):
    return pl.CostEstimate(
        flops=2 * products * size**3, bytes_accessed=bytes_accessed, transcendentals=0
    )


def place():
    position = lax.axis_index("seg")
    return position % 2, position // 2


def limit(mebibytes):
    return pltpu.CompilerParams(vmem_limit_bytes=mebibytes * MIB)


def live(dim, size):
    rows = lax.broadcasted_iota(jnp.int32, (size, size), 0) < dim
    columns = lax.broadcasted_iota(jnp.int32, (size, size), 1) < dim
    return rows & columns


def in_hbm(array):
    return pltpu.with_memory_space_constraint(array, pltpu.HBM)


def split_kernel(gauge, state, own, other, gauge_here, state_here, sems):
    core = place()[0]
    arrivals = [
        pltpu.make_async_copy(gauge, gauge_here, sems.at[0]),
        pltpu.make_async_copy(state, state_here, sems.at[1]),
    ]
    for copy in arrivals:
        copy.start()
    for copy in arrivals:
        copy.wait()
    own[0] = gauge_here[core].astype(BF16)
    own[1] = state_here[core]
    other[0] = gauge_here[1 - core].astype(BF16)
    other[1] = state_here[1 - core]


def table_kernel(charge_far, mask_far, dims_far, left, cells, to_left, to_right, table, charge,
                 mask, dims, sems, cross_sems):
    channels, size = left.shape[1], left.shape[2]
    arrivals = [
        pltpu.make_async_copy(charge_far, charge, sems.at[0]),
        pltpu.make_async_copy(mask_far, mask, sems.at[1]),
        pltpu.make_async_copy(dims_far, dims, sems.at[2]),
    ]
    for copy in arrivals:
        copy.start()
    for copy in arrivals:
        copy.wait()
    ups, downs, rest = jnp.int32(0), jnp.int32(0), jnp.int32(0)
    for w in range(channels):
        up, down = charge[w] == 1, charge[w] == -1
        middle = QUARTER + rest
        table[0, jnp.where(up, ups, jnp.where(down, channels - QUARTER + downs, middle))] = w
        table[1, jnp.where(down, downs, jnp.where(up, channels - QUARTER + ups, middle))] = w
        ups = ups + up.astype(jnp.int32)
        downs = downs + down.astype(jnp.int32)
        rest = rest + jnp.where(up | down, 0, 1)
    crossings = []
    for s in range(2):
        for j in range(QUARTER):
            w = table[s, channels - QUARTER + j]
            crossings.append(
                pltpu.make_async_copy(
                    left.at[s, w], (to_left, to_right)[s].at[j], cross_sems.at[s, j]
                )
            )
            crossings[-1].start()
    for s in range(2):
        for j in range(channels):
            table[2 + s, j] = mask[s, table[s, j]]
        cells[s] = jnp.where(live(dims[s], size), 1.0, 0.0).astype(BF16)
    for copy in crossings:
        copy.wait()


def sort_kernel(masked, table, source, target, sems):
    channels = source.shape[1]

    def copy(s, j):
        return pltpu.make_async_copy(
            source.at[s, table[s, j]], target.at[s, j], sems.at[s, j]
        )

    for s in range(2):
        for j in range(channels):
            copy(s, j).start()
    for s in range(2):
        for j in range(channels):
            copy(s, j).wait()
            if masked:
                @pl.when(table[2 + s, j] == 0)
                def _():
                    target[s, j] = jnp.zeros(target.shape[2:], target.dtype)


def joined(later, earlier):
    return later.astype(F32) + earlier.astype(F32) + dot(later, earlier)


def pair_kernel(own, got, after, out):
    core = place()[0]

    @pl.when(core == 0)
    def _():
        out[...] = joined(got[0], own[0]).astype(BF16)

    @pl.when(core == 1)
    def _():
        out[...] = joined(own[0], got[0]).astype(BF16)


def four_kernel(own, got, after, out):
    chip = place()[1]

    @pl.when(chip % 2 == 0)
    def _():
        out[...] = joined(got[...], own[...]).astype(BF16)

    @pl.when(chip % 2 == 1)
    def _():
        out[...] = joined(own[...], got[...]).astype(BF16)


def state_kernel(cells, own, got, near, far, *refs):
    x_own, x_other, pair = refs[-3:]
    core, chip = place()
    size = x_own.shape[0]
    pair[core] = own[...]
    pair[1 - core] = got[...]
    field = jnp.concatenate([pair[0, 1], pair[1, 1]], axis=1)
    wide = field.astype(F32)
    wide = wide + dot(far[...], field)
    near_here = jnp.where(chip != 0, near[...].astype(F32), 0.0).astype(BF16)
    wide = wide + dot(near_here, wide.astype(BF16))
    wide = wide + dot(pair[0, 0], wide.astype(BF16))
    earlier, later = wide[:, :size], wide[:, size:]
    later = later + dot(pair[1, 0], later.astype(BF16))
    alive = cells[core] != 0
    first = jnp.where(alive, earlier, 0.0).astype(BF16)
    second = jnp.where(alive, later, 0.0).astype(BF16)
    x_own[...] = jnp.where(core == 0, first, second)
    x_other[...] = jnp.where(core == 0, second, first)


def spread(parts, s, blocks, field, first, last):
    size = field.shape[0]
    rows = blocks[s, first:last].reshape((last - first) * size, size)
    result = dot(rows, field).astype(BF16)
    for j in range(first, last):
        at = (j - first) * size
        parts[s, :, j * size : (j + 1) * size] = result[at : at + size]


def folded(parts, s, blocks, first, last):
    size = blocks.shape[-1]
    rows = blocks[s, first:last].reshape((last - first) * size, size)
    return dot(parts[s, :, first * size : last * size], rows)


def own_kernel(x_own, x_got, left, right, table_far, acc, env, x_here, parts, blocks, table,
               table_sem, out_sems):
    core = place()[0]
    channels, size = left.shape[1], left.shape[2]
    cross = channels - QUARTER
    fetch = pltpu.make_async_copy(table_far, table, table_sem.at[0])
    fetch.start()
    x_here[core] = x_own[...]
    x_here[1 - core] = x_got[...]

    def send(s, j):
        target = 1 - s if j < QUARTER else s
        return pltpu.make_async_copy(
            blocks.at[s, j], env.at[0, target, table[s, j]], out_sems.at[s, j]
        )

    for s in range(2):
        field = x_here[s]
        turned = field.T
        spread(parts, s, left, field, 0, cross)
        result = dot(turned, parts[s, :, : cross * size]).astype(BF16)
        for j in range(cross):
            blocks[s, j] = result[:, j * size : (j + 1) * size]
        if s == 0:
            fetch.wait()
        for j in range(cross):
            send(s, j).start()
    for s in range(2):
        spread(parts, s, left, x_here[1 - s], cross, channels)
        acc[s] = folded(parts, s, right, QUARTER, channels)
    for s in range(2):
        for j in range(cross):
            send(s, j).wait()


def image_kernel(cells, x_here, side_same, side_cross, left_side, right_side, acc, v_first,
                 v_second, sums, x_side, parts):
    core = place()[0]
    x_side[1 - core] = side_same[...]
    x_side[core] = side_cross[...]
    total = []
    for s in range(2):
        spread(parts, s, left_side, x_side[s], 0, QUARTER)
        image = acc[s] + folded(parts, s, right_side, 0, QUARTER)
        image = jnp.where(cells[s] != 0, image, 0.0).astype(BF16)
        (v_first, v_second)[s][...] = image
        total.append(image)

    def whole(values):
        return jnp.sum(jnp.sum(values, axis=0, keepdims=True), axis=1, keepdims=True)

    x_wide = [x_here[s].astype(F32) for s in range(2)]
    v_wide = [total[s].astype(F32) for s in range(2)]
    norm = whole(x_wide[0] * x_wide[0] + x_wide[1] * x_wide[1])
    correlation = whole(x_wide[0] * v_wide[0] + x_wide[1] * v_wide[1])
    ratio = jnp.where(norm > 0.0, correlation / jnp.where(norm > 0.0, norm, 1.0), 0.0)
    apart = [v_wide[s] - ratio * x_wide[s] for s in range(2)]
    spread_of = whole(apart[0] * apart[0] + apart[1] * apart[1])
    lane = lax.broadcasted_iota(jnp.int32, sums.shape, 1)
    row = jnp.where(lane == 0, norm, jnp.where(lane == 1, correlation, 0.0))
    row = jnp.where(lane == 2, ratio, jnp.where(lane == 3, spread_of, row))
    sums[...] = row


def krylov_kernel(total_cells, cells, sums, x_here, x_side, v_first, v_second, v_left, v_right,
                  left_up, left_down, table_far, charge_far, mask_far, left, right, env_in,
                  krylov, env, rayleigh, left_here, right_here, fields, parts, side_parts,
                  blocks, table, charge, mask, sems, small_sems, out_sems):
    channels, size = left.shape[1], left.shape[2]
    half = channels // 2
    steps = [(side, s, h) for s in range(2) for side in range(2) for h in range(2)]

    def load(step):
        side, s, h = steps[step]
        source, target = ((left, left_here), (right, right_here))[side]
        span = pl.ds(h * half, half)
        return pltpu.make_async_copy(source.at[s, span], target.at[s, span], sems.at[step])

    small = [
        pltpu.make_async_copy(table_far, table, small_sems.at[0]),
        pltpu.make_async_copy(charge_far, charge, small_sems.at[1]),
        pltpu.make_async_copy(mask_far, mask, small_sems.at[2]),
    ]
    for copy in small:
        copy.start()
    ahead = 3
    for step in range(ahead):
        load(step).start()

    column = [jnp.sum(sums[:, i : i + 1], axis=0, keepdims=True) for i in range(2)]
    ratio = column[1] / column[0]
    apart = ratio - sums[:, 2:3]
    spread_of = jnp.sum(sums[:, 3:4] + apart * apart * sums[:, 0:1], axis=0, keepdims=True)
    inverse = 1.0 / jnp.sqrt(spread_of * (1.0 / total_cells) + 1e-06)
    rayleigh[0] = ratio[0, 0]

    def scaled(v, x):
        return ((v.astype(F32) - ratio * x.astype(F32)) * inverse).astype(BF16)

    fields[0] = scaled(v_left[...], x_side[0])
    fields[1] = scaled(v_first[...], x_here[0])
    fields[2] = scaled(v_second[...], x_here[1])
    fields[3] = scaled(v_right[...], x_side[1])

    def send(s, j):
        return pltpu.make_async_copy(
            blocks.at[s, j], env.at[0, s, table[s, j]], out_sems.at[s, j]
        )

    for s in range(2):
        turned = x_side[s].T
        arriving = (left_up, left_down)[s]
        lx = dot(arriving[...].reshape(QUARTER * size, size), x_side[s]).astype(BF16)
        for j in range(QUARTER):
            side_parts[:, j * size : (j + 1) * size] = lx[j * size : (j + 1) * size]
        result = dot(turned, side_parts[...]).astype(BF16)
        for j in range(QUARTER):
            blocks[s, j] = result[:, j * size : (j + 1) * size]
    for copy in small:
        copy.wait()
    for s in range(2):
        for j in range(QUARTER):
            send(s, j).start()

    image = None
    for step, (side, s, h) in enumerate(steps):
        load(step).wait()
        if step + ahead < len(steps):
            load(step + ahead).start()
        span = range(h * half, (h + 1) * half)
        if side == 0:
            for w in span:
                part = dot(left_here[s, w], fields[s + 1 - charge[w]])
                part = part * mask[s, w].astype(F32)
                parts[:, w * size : (w + 1) * size] = part.astype(BF16)
        else:
            rows = right_here[s, h * half : (h + 1) * half].reshape(half * size, size)
            product = dot(parts[:, h * half * size : (h + 1) * half * size], rows)
            image = product if h == 0 else image + product
            if h == 1:
                krylov[0, s] = jnp.where(cells[s] != 0, image, 0.0).astype(BF16)
    for s in range(2):
        for j in range(QUARTER):
            send(s, j).wait()


def local(state_blocks, gauge_offset, left_env, right_env, mpo_mask, charge, block_dims):
    size = state_blocks.shape[-1]
    channels = left_env.shape[2]
    segments = lax.axis_size("seg")
    groups = lax.axis_size("sec")
    block = (size, size)

    def at(segment, group):
        return segment * groups + group

    every = range(groups)
    swap = [(at(k, i), at(k ^ 1, i)) for k in range(segments) for i in every]
    chip_pairs = [
        (at(2 * a + r, i), at(2 * b + r, i))
        for a, b in ((0, 1), (1, 0), (2, 3)) for r in range(2) for i in every
    ]
    far_pairs = [
        (at(2 * a + r, i), at(2 * b + r, i))
        for a, b in ((1, 2), (0, 3)) for r in range(2) for i in every
    ]
    same, cross = [], []
    for c in range(segments // 2):
        for i in every:
            if i > 0:
                same.append((at(2 * c, i), at(2 * c, i - 1)))
                cross.append((at(2 * c, i), at(2 * c + 1, i - 1)))
            if i < groups - 1:
                same.append((at(2 * c + 1, i), at(2 * c + 1, i + 1)))
                cross.append((at(2 * c + 1, i), at(2 * c, i + 1)))
    leftward = [(i, i - 1) for i in range(1, groups)]
    rightward = [(i, i + 1) for i in range(groups - 1)]

    left, right = in_hbm(left_env[0]), in_hbm(right_env[0])
    whole = (2, channels) + block
    own, other = pl.pallas_call(
        split_kernel,
        out_shape=[jax.ShapeDtypeStruct((2,) + block, BF16)] * 2,
        in_specs=anywhere(2),
        out_specs=vmem(2),
        scratch_shapes=[
            pltpu.VMEM((2,) + block, F32),
            pltpu.VMEM((2,) + block, BF16),
            pltpu.SemaphoreType.DMA((2,)),
        ],
        compiler_params=limit(4),
        cost_estimate=cost(0, size, 2 * MIB),
    )(in_hbm(gauge_offset[0]), in_hbm(state_blocks[0]))
    got = lax.ppermute(other, AXES, swap)
    cells, to_left, to_right, table = pl.pallas_call(
        table_kernel,
        out_shape=[
            jax.ShapeDtypeStruct((2,) + block, BF16),
            jax.ShapeDtypeStruct((QUARTER,) + block, BF16),
            jax.ShapeDtypeStruct((QUARTER,) + block, BF16),
            jax.ShapeDtypeStruct((4, channels), jnp.int32),
        ],
        in_specs=anywhere(4),
        out_specs=vmem(3) + smem(1),
        scratch_shapes=[
            pltpu.SMEM(charge.shape, jnp.int32),
            pltpu.SMEM(mpo_mask.shape, jnp.int32),
            pltpu.SMEM(block_dims.shape, jnp.int32),
            pltpu.SemaphoreType.DMA((3,)),
            pltpu.SemaphoreType.DMA((2, QUARTER)),
        ],
        compiler_params=limit(4),
        cost_estimate=cost(0, size, 2 * MIB),
    )(in_hbm(charge), in_hbm(mpo_mask), in_hbm(block_dims), left)
    left_up = lax.ppermute(to_right, "sec", rightward)
    left_down = lax.ppermute(to_left, "sec", leftward)

    def sort(masked, source):
        return pl.pallas_call(
            functools.partial(sort_kernel, masked),
            out_shape=jax.ShapeDtypeStruct(whole, BF16),
            in_specs=smem(1) + anywhere(1),
            out_specs=vmem(1)[0],
            scratch_shapes=[pltpu.SemaphoreType.DMA((2, channels))],
            compiler_params=limit(4),
            cost_estimate=cost(0, size, 8 * MIB),
        )(table, source)

    pair = pl.pallas_call(
        pair_kernel,
        out_shape=jax.ShapeDtypeStruct(block, BF16),
        in_specs=vmem(2) + anywhere(1),
        out_specs=vmem(1)[0],
        compiler_params=limit(4),
        cost_estimate=cost(1, size, MIB),
    )(own, got, cells)
    near = lax.ppermute(pair, AXES, chip_pairs)
    left_sorted = sort(False, left)
    four = pl.pallas_call(
        four_kernel,
        out_shape=jax.ShapeDtypeStruct(block, BF16),
        in_specs=vmem(2) + anywhere(1),
        out_specs=vmem(1)[0],
        compiler_params=limit(4),
        cost_estimate=cost(1, size, MIB),
    )(pair, near, left_sorted)
    far = lax.ppermute(four, AXES, far_pairs)
    right_sorted = sort(True, right)

    x_own, x_other = pl.pallas_call(
        state_kernel,
        out_shape=[jax.ShapeDtypeStruct(block, BF16)] * 2,
        in_specs=vmem(5) + anywhere(3),
        out_specs=vmem(2),
        scratch_shapes=[pltpu.VMEM((2, 2) + block, BF16)],
        compiler_params=limit(6),
        cost_estimate=cost(8, size, 2 * MIB),
    )(cells, own, got, near, far, right_sorted, left_up, left_down)
    x_got = lax.ppermute(x_other, AXES, swap)
    side_same = lax.ppermute(x_own, AXES, same)
    side_cross = lax.ppermute(x_other, AXES, cross)

    acc, env, x_here = pl.pallas_call(
        own_kernel,
        out_shape=[
            jax.ShapeDtypeStruct((2,) + block, F32),
            pltpu.HBM((1, 2, channels) + block, BF16),
            jax.ShapeDtypeStruct((2,) + block, BF16),
        ],
        in_specs=vmem(4) + anywhere(1),
        out_specs=vmem(1) + anywhere(1) + vmem(1),
        scratch_shapes=[
            pltpu.VMEM((2, size, channels * size), BF16),
            pltpu.VMEM((2, channels - QUARTER) + block, BF16),
            pltpu.SMEM((4, channels), jnp.int32),
            pltpu.SemaphoreType.DMA((1,)),
            pltpu.SemaphoreType.DMA((2, channels - QUARTER)),
        ],
        compiler_params=limit(12),
        cost_estimate=cost(88, size, 12 * MIB),
    )(x_own, x_got, left_sorted, right_sorted, table)

    v_first, v_second, sums, x_side = pl.pallas_call(
        image_kernel,
        out_shape=[
            jax.ShapeDtypeStruct(block, BF16),
            jax.ShapeDtypeStruct(block, BF16),
            jax.ShapeDtypeStruct((groups, 128), F32),
            jax.ShapeDtypeStruct((2,) + block, BF16),
        ],
        in_specs=vmem(7),
        out_specs=vmem(4),
        scratch_shapes=[pltpu.VMEM((2, size, QUARTER * size), BF16)],
        compiler_params=limit(10),
        cost_estimate=cost(16, size, 4 * MIB),
    )(cells, x_here, side_same, side_cross, left_sorted, right_sorted, acc)
    v_right = lax.ppermute(v_first, "sec", leftward)
    v_left = lax.ppermute(v_second, "sec", rightward)
    sums = lax.all_to_all(sums, "sec", 0, 0)

    total_cells = float(groups * 2 * size * size)
    krylov, env, rayleigh = pl.pallas_call(
        lambda *refs: krylov_kernel(total_cells, *refs),
        out_shape=[
            jax.ShapeDtypeStruct((1, 2) + block, BF16),
            jax.ShapeDtypeStruct((1, 2, channels) + block, BF16),
            jax.ShapeDtypeStruct((1,), F32),
        ],
        in_specs=vmem(10) + anywhere(6),
        out_specs=vmem(1) + anywhere(1) + smem(1),
        scratch_shapes=[
            pltpu.VMEM(whole, BF16),
            pltpu.VMEM(whole, BF16),
            pltpu.VMEM((4,) + block, BF16),
            pltpu.VMEM((size, channels * size), BF16),
            pltpu.VMEM((size, QUARTER * size), BF16),
            pltpu.VMEM((2, QUARTER) + block, BF16),
            pltpu.SMEM((4, channels), jnp.int32),
            pltpu.SMEM(charge.shape, jnp.int32),
            pltpu.SMEM(mpo_mask.shape, jnp.int32),
            pltpu.SemaphoreType.DMA((8,)),
            pltpu.SemaphoreType.DMA((3,)),
            pltpu.SemaphoreType.DMA((2, QUARTER)),
        ],
        input_output_aliases={15: 1},
        compiler_params=limit(32),
        cost_estimate=cost(80, size, 12 * MIB),
    )(cells, sums, x_here, x_side, v_first, v_second, v_left, v_right, left_up, left_down,
      table, in_hbm(charge), in_hbm(mpo_mask), left, right, env)
    return krylov, env, rayleigh


def solution(mesh):
    return jax.shard_map(
        local,
        mesh=mesh,
        in_specs=(
            P("seg", "sec", None, None),
            P("seg", "sec", None, None),
            P("seg", "sec", None, None, None),
            P("seg", "sec", None, None, None),
            P("sec", None),
            P(),
            P("sec"),
        ),
        out_specs=(P("seg", "sec", None, None), P("seg", "sec", None, None, None), P("seg")),
        check_vma=False,
    )
```

time: 334 us -> 79.7 us (0.24)
  the two profiles are of different devices: /device:TPU:110 before, /device:TPU:1 now
where the time goes in v1:
time: 79.7 us; the launch traced here: 78.7 us
  starting transfers between devices  27.6 us (35%)
  Pallas kernels  26 us (33%)
  blocking collectives  23.7 us (30%)
  between operations  0.97 us (1%)
    all_to_all x1, blocking collectives, local(): sums = lax.all_to_all(sums, 'sec', 0, 0)  23.7 us
    pallas_call x1, Pallas kernels, local(): pl.pallas_call(lambda *refs: krylov_kernel(total_cells, *refs), out_shape...  8.53 us
    pallas_call x2, Pallas kernels, sort(): pl.pallas_call(functools.partial(sort_kernel, masked), out_shape=jax.Shap...  6.17 us
    pallas_call x1, Pallas kernels, local(): pl.pallas_call(own_kernel, out_shape=[jax.ShapeDtypeStruct((2,) + block,...  4.84 us
    ppermute x1, starting transfers between devices, local(): far = lax.ppermute(four, AXES, far_pairs)  4.65 us
    ppermute x1, starting transfers between devices, local(): v_left = lax.ppermute(v_second, 'sec', rightward)  3.99 us
    ppermute x1, starting transfers between devices, local(): side_cross = lax.ppermute(x_other, AXES, cross)  3.89 us
    ppermute x1, starting transfers between devices, local(): got = lax.ppermute(other, AXES, swap)  3.33 us
  transfers between devices with their start and end apart: 10, of which 1 were waited for; matrix products, arithmetic and copies ran while one was open for 0% of the time, Pallas kernels for 18%

profile of v1, /device:TPU:1, one launch (start us, length us, event | category | flops | bytes accessed | tf_op | source)
XLA Modules:
  0.0 78.7 jit_solution(3855136174680103593)
XLA Ops:
  0.6 1.2 %shard_map.95 = (bf16[2,256,256]{2,1,0:T(8,128)(2,1)S(1)}, bf16[2,256,256]{2,1,0:T(8,128)(2,1)S(1)}) custom-call(f32[2,256,256]{2,1,0:T(8,128)} %bitcast.15, bf16[2,256,256]{2,1,0:T(8,128)(2,1)} %bitcast.16), custom_call_target="tpu_custom_call" | custom-call | bytes 2097152 | tf_op jit(solution)/shard_map/pallas_call | solution.py:379
  1.8 3.3 %collective-permute-start = (bf16[2,256,256]{2,1,0:T(8,128)(2,1)S(1)}, bf16[2,256,256]{2,1,0:T(8,128)(2,1)S(1)}, u32[]{:S(2)}, u32[]{:S(2)}) collective-permute-start(bf16[2,256,256]{2,1,0:T(8,128)(2,1)S(1)} %get-tuple-element.20), channel_id=1, source_target_pairs={{0,32},{1,33},{2,34},{3,35},{4,36},{5,37},{6,38},{7,39},{8,40},{9,... | collective-permute-start | bytes 786440 | tf_op jit(solution)/shard_map/ppermute | solution.py:392
  5.1 2.9 %shard_map.94 = (bf16[2,256,256]{2,1,0:T(8,128)(2,1)S(1)}, bf16[4,256,256]{2,1,0:T(8,128)(2,1)S(1)}, bf16[4,256,256]{2,1,0:T(8,128)(2,1)S(1)}, s32[4,16]{1,0:T(4,128)S(1)}) custom-call(s32[16]{0:T(128)} %refs_11_.1, s32[2,16]{1,0:T(2,128)} %refs_12_.1, s32[2]{0:T(128)} %dims_far.1, bf16[2,16,256,256]{3,2,1,0:T(8,128)(2,1)} %bitcast.10), custom_call_target="tpu_custom_call" | custom-call | bytes 2097152 | tf_op jit(solution)/shard_map/pallas_call | solution.py:393
  8.0 1.4 %collective-permute-start.3 = (bf16[4,256,256]{2,1,0:T(8,128)(2,1)S(1)}, bf16[4,256,256]{2,1,0:T(8,128)(2,1)S(1)}, u32[]{:S(2)}, u32[]{:S(2)}) collective-permute-start(bf16[4,256,256]{2,1,0:T(8,128)(2,1)S(1)} %get-tuple-element.22), channel_id=1, source_target_pairs={{0,1},{1,2},{2,3},{3,4},{4,5},{5,6},{6,7},{7,8},{8,9},{9,10},{10,1... | collective-permute-start | bytes 1572872 | tf_op jit(solution)/shard_map/ppermute | solution.py:413
  9.4 1.3 %collective-permute-start.4 = (bf16[4,256,256]{2,1,0:T(8,128)(2,1)S(1)}, bf16[4,256,256]{2,1,0:T(8,128)(2,1)S(1)}, u32[]{:S(2)}, u32[]{:S(2)}) collective-permute-start(bf16[4,256,256]{2,1,0:T(8,128)(2,1)S(1)} %get-tuple-element.23), channel_id=1, source_target_pairs={{1,0},{2,1},{3,2},{4,3},{5,4},{6,5},{7,6},{8,7},{9,8},{10,9},{11,1... | collective-permute-start | bytes 1572872 | tf_op jit(solution)/shard_map/ppermute | solution.py:414
  10.7 0.0 collective-permute-done.got
  10.7 0.2 shard_map.96.own
  10.9 3.2 %collective-permute-start.1 = (bf16[256,256]{1,0:T(8,128)(2,1)S(1)}, bf16[256,256]{1,0:T(8,128)(2,1)S(1)}, u32[]{:S(2)}, u32[]{:S(2)}) collective-permute-start(bf16[256,256]{1,0:T(8,128)(2,1)S(1)} %shard_map.96.own), channel_id=1, source_target_pairs={{0,64},{1,65},{2,66},{3,67},{4,68},{5,69},{6,70},{7,71},{8,72},{9,... | collective-permute-start | bytes 393224 | tf_op jit(solution)/shard_map/ppermute | solution.py:435
  14.2 3.1 %shard_map.97.after.left.left_side = bf16[2,16,256,256]{3,2,1,0:T(8,128)(2,1)S(1)} custom-call(s32[4,16]{1,0:T(4,128)S(1)} %get-tuple-element.21.table.table_far.refs_10_, bf16[2,16,256,256]{3,2,1,0:T(8,128)(2,1)} %bitcast.11), custom_call_target="tpu_custom_call" | custom-call | bytes 8388608 | tf_op jit(solution)/shard_map/pallas_call | solution.py:417
  17.3 0.4 collective-permute-done.1.got.near
  17.6 0.2 shard_map.98
  17.8 4.6 %collective-permute-start.2 = (bf16[256,256]{1,0:T(8,128)(2,1)S(1)}, bf16[256,256]{1,0:T(8,128)(2,1)S(1)}, u32[]{:S(2)}, u32[]{:S(2)}) collective-permute-start(bf16[256,256]{1,0:T(8,128)(2,1)S(1)} %shard_map.98), channel_id=1, source_target_pairs={{64,128},{65,129},{66,130},{67,131},{68,132},{69,133},{70,134},{71... | collective-permute-start | bytes 393224 | tf_op jit(solution)/shard_map/ppermute | solution.py:445
  22.5 3.1 %shard_map.99.refs_0_.right.right_side = bf16[2,16,256,256]{3,2,1,0:T(8,128)(2,1)S(1)} custom-call(s32[4,16]{1,0:T(4,128)S(1)} %get-tuple-element.21.table.table_far.refs_10_, bf16[2,16,256,256]{3,2,1,0:T(8,128)(2,1)} %bitcast.13), custom_call_target="tpu_custom_call" | custom-call | bytes 8388608 | tf_op jit(solution)/shard_map/pallas_call | solution.py:417
  25.6 0.0 collective-permute-done.3.refs_1_.refs_8_
  25.6 0.0 collective-permute-done.4.refs_2_.refs_9_
  25.6 0.0 collective-permute-done.2.far
  25.6 0.9 %shard_map.100 = (bf16[256,256]{1,0:T(8,128)(2,1)S(1)}, bf16[256,256]{1,0:T(8,128)(2,1)S(1)}) custom-call(bf16[2,256,256]{2,1,0:T(8,128)(2,1)S(1)} %get-tuple-element.18.after.cells.refs_0_, bf16[2,256,256]{2,1,0:T(8,128)(2,1)S(1)} %get-tuple-element.19.own, bf16[2,256,256]{2,1,0:T(8,128)(2,1)S(1)} %collective-permute-done.got, ...), custom_call_target="tpu_custom_call" | custom-call | flops 268435456 | bytes 2097152 | tf_op jit(solution)/shard_map/pallas_call | solution.py:448
  26.5 1.5 %collective-permute-start.5 = (bf16[256,256]{1,0:T(8,128)(2,1)S(1)}, bf16[256,256]{1,0:T(8,128)(2,1)S(1)}, u32[]{:S(2)}, u32[]{:S(2)}) collective-permute-start(bf16[256,256]{1,0:T(8,128)(2,1)S(1)} %get-tuple-element.25), channel_id=1, source_target_pairs={{0,32},{1,33},{2,34},{3,35},{4,36},{5,37},{6,38},{7,39},{8,40},{9,... | collective-permute-start | bytes 393224 | tf_op jit(solution)/shard_map/ppermute | solution.py:457
  28.0 3.9 %collective-permute-start.7 = (bf16[256,256]{1,0:T(8,128)(2,1)S(1)}, bf16[256,256]{1,0:T(8,128)(2,1)S(1)}, u32[]{:S(2)}, u32[]{:S(2)}) collective-permute-start(bf16[256,256]{1,0:T(8,128)(2,1)S(1)} %get-tuple-element.25), channel_id=1, source_target_pairs={{32,1},{1,32},{33,2},{2,33},{34,3},{3,34},{35,4},{4,35},{36,5},{5,... | collective-permute-start | bytes 393224 | tf_op jit(solution)/shard_map/ppermute | solution.py:459
  31.9 3.1 %collective-permute-start.6 = (bf16[256,256]{1,0:T(8,128)(2,1)S(1)}, bf16[256,256]{1,0:T(8,128)(2,1)S(1)}, u32[]{:S(2)}, u32[]{:S(2)}) collective-permute-start(bf16[256,256]{1,0:T(8,128)(2,1)S(1)} %get-tuple-element.24.x_own), channel_id=1, source_target_pairs={{32,33},{1,0},{33,34},{2,1},{34,35},{3,2},{35,36},{4,3},{36,37},{5... | collective-permute-start | bytes 393224 | tf_op jit(solution)/shard_map/ppermute | solution.py:458
  35.0 0.0 collective-permute-done.5.x_got
  35.0 4.8 %shard_map.101 = (f32[2,256,256]{2,1,0:T(8,128)S(1)}, bf16[1,2,16,256,256]{4,3,2,1,0:T(8,128)(2,1)}, bf16[2,256,256]{2,1,0:T(8,128)(2,1)S(1)}) custom-call(bf16[256,256]{1,0:T(8,128)(2,1)S(1)} %get-tuple-element.24.x_own, bf16[256,256]{1,0:T(8,128)(2,1)S(1)} %collective-permute-done.5.x_got, bf16[2,16,256,256]{3,2,1,0:T(8,128)(2,1)S(1)} %shard_map.97.after.left.left_side, ...), custom_call_target="tpu_custom_call" | custom-call | flops 2952790016 | bytes 12582912 | tf_op jit(solution)/shard_map/pallas_call | solution.py:461
  39.8 0.0 collective-permute-done.6.side_same
  39.8 0.0 collective-permute-done.7.side_cross
  39.8 1.2 %shard_map.102 = (bf16[256,256]{1,0:T(8,128)(2,1)S(1)}, bf16[256,256]{1,0:T(8,128)(2,1)S(1)}, f32[32,128]{1,0:T(8,128)S(1)}, bf16[2,256,256]{2,1,0:T(8,128)(2,1)S(1)}) custom-call(bf16[2,256,256]{2,1,0:T(8,128)(2,1)S(1)} %get-tuple-element.18.after.cells.refs_0_, bf16[2,256,256]{2,1,0:T(8,128)(2,1)S(1)} %get-tuple-element.26.x_here.refs_2_, ...), custom_call_target="tpu_custom_call" | custom-call | flops 536870912 | bytes 4194304 | tf_op jit(solution)/shard_map/pallas_call | solution.py:481
  41.0 1.3 %collective-permute-start.9 = (bf16[256,256]{1,0:T(8,128)(2,1)S(1)}, bf16[256,256]{1,0:T(8,128)(2,1)S(1)}, u32[]{:S(2)}, u32[]{:S(2)}) collective-permute-start(bf16[256,256]{1,0:T(8,128)(2,1)S(1)} %get-tuple-element.30.refs_4_), channel_id=1, source_target_pairs={{1,0},{2,1},{3,2},{4,3},{5,4},{6,5},{7,6},{8,7},{9,8},{10,9},{11,1... | collective-permute-start | bytes 393224 | tf_op jit(solution)/shard_map/ppermute | solution.py:495
  42.3 4.0 %collective-permute-start.8 = (bf16[256,256]{1,0:T(8,128)(2,1)S(1)}, bf16[256,256]{1,0:T(8,128)(2,1)S(1)}, u32[]{:S(2)}, u32[]{:S(2)}) collective-permute-start(bf16[256,256]{1,0:T(8,128)(2,1)S(1)} %get-tuple-element.31.refs_5_), channel_id=1, source_target_pairs={{0,1},{1,2},{2,3},{3,4},{4,5},{5,6},{6,7},{7,8},{8,9},{9,10},{10,1... | collective-permute-start | bytes 393224 | tf_op jit(solution)/shard_map/ppermute | solution.py:496
  46.3 23.7 %all_to_all.11 = f32[32,1,128]{2,1,0:T(1,128)S(1)} all-to-all(f32[32,1,128]{2,1,0:T(1,128)S(1)} %bitcast.9), channel_id=1, replica_groups=mesh['seg'=8,'sec'=32] {'sec'}, dimensions={0} | all-to-all | bytes 32768 | tf_op jit(solution)/shard_map/all_to_all | solution.py:497
  70.0 0.0 collective-permute-done.9.refs_7_
  70.0 0.0 collective-permute-done.8.refs_6_
  70.0 8.5 %shard_map.103 = (bf16[1,2,256,256]{3,2,1,0:T(8,128)(2,1)}, bf16[1,2,16,256,256]{4,3,2,1,0:T(8,128)(2,1)}, f32[1]{0:T(128)}) custom-call(bf16[2,256,256]{2,1,0:T(8,128)(2,1)S(1)} %get-tuple-element.18.after.cells.refs_0_, f32[32,128]{1,0:T(8,128)S(1)} %bitcast.8, ...), custom_call_target="tpu_custom_call", output_to_operand_aliasing={{1}: (15, {})} | custom-call | flops 2684354560 | bytes 12582912 | tf_op jit(solution)/shard_map/pallas_call | solution.py:500
Async XLA Ops:
  1.8 8.9 %collective-permute-start = (bf16[2,256,256]{2,1,0:T(8,128)(2,1)S(1)}, bf16[2,256,256]{2,1,0:T(8,128)(2,1)S(1)}, u32[]{:S(2)}, u32[]{:S(2)}) collective-permute-start(bf16[2,256,256]{2,1,0:T(8,128)(2,1)S(1)} %get-tuple-element.20), channel_id=1, source_target_pairs={{0,32},{1,33},{2,34},{3,35},{4,36},{5,37},{6,38},{7,39},{8,40},{9,... | collective-permute-start | bytes 786440 | tf_op jit(solution)/shard_map/ppermute | solution.py:392
  8.0 17.6 %collective-permute-start.3 = (bf16[4,256,256]{2,1,0:T(8,128)(2,1)S(1)}, bf16[4,256,256]{2,1,0:T(8,128)(2,1)S(1)}, u32[]{:S(2)}, u32[]{:S(2)}) collective-permute-start(bf16[4,256,256]{2,1,0:T(8,128)(2,1)S(1)} %get-tuple-element.22), channel_id=1, source_target_pairs={{0,1},{1,2},{2,3},{3,4},{4,5},{5,6},{6,7},{7,8},{8,9},{9,10},{10,1... | collective-permute-start | bytes 1572872 | tf_op jit(solution)/shard_map/ppermute | solution.py:413
  9.4 16.2 %collective-permute-start.4 = (bf16[4,256,256]{2,1,0:T(8,128)(2,1)S(1)}, bf16[4,256,256]{2,1,0:T(8,128)(2,1)S(1)}, u32[]{:S(2)}, u32[]{:S(2)}) collective-permute-start(bf16[4,256,256]{2,1,0:T(8,128)(2,1)S(1)} %get-tuple-element.23), channel_id=1, source_target_pairs={{1,0},{2,1},{3,2},{4,3},{5,4},{6,5},{7,6},{8,7},{9,8},{10,9},{11,1... | collective-permute-start | bytes 1572872 | tf_op jit(solution)/shard_map/ppermute | solution.py:414
  10.9 6.7 %collective-permute-start.1 = (bf16[256,256]{1,0:T(8,128)(2,1)S(1)}, bf16[256,256]{1,0:T(8,128)(2,1)S(1)}, u32[]{:S(2)}, u32[]{:S(2)}) collective-permute-start(bf16[256,256]{1,0:T(8,128)(2,1)S(1)} %shard_map.96.own), channel_id=1, source_target_pairs={{0,64},{1,65},{2,66},{3,67},{4,68},{5,69},{6,70},{7,71},{8,72},{9,... | collective-permute-start | bytes 393224 | tf_op jit(solution)/shard_map/ppermute | solution.py:435
  17.8 7.8 %collective-permute-start.2 = (bf16[256,256]{1,0:T(8,128)(2,1)S(1)}, bf16[256,256]{1,0:T(8,128)(2,1)S(1)}, u32[]{:S(2)}, u32[]{:S(2)}) collective-permute-start(bf16[256,256]{1,0:T(8,128)(2,1)S(1)} %shard_map.98), channel_id=1, source_target_pairs={{64,128},{65,129},{66,130},{67,131},{68,132},{69,133},{70,134},{71... | collective-permute-start | bytes 393224 | tf_op jit(solution)/shard_map/ppermute | solution.py:445
  26.5 8.5 %collective-permute-start.5 = (bf16[256,256]{1,0:T(8,128)(2,1)S(1)}, bf16[256,256]{1,0:T(8,128)(2,1)S(1)}, u32[]{:S(2)}, u32[]{:S(2)}) collective-permute-start(bf16[256,256]{1,0:T(8,128)(2,1)S(1)} %get-tuple-element.25), channel_id=1, source_target_pairs={{0,32},{1,33},{2,34},{3,35},{4,36},{5,37},{6,38},{7,39},{8,40},{9,... | collective-permute-start | bytes 393224 | tf_op jit(solution)/shard_map/ppermute | solution.py:457
  28.0 11.9 %collective-permute-start.7 = (bf16[256,256]{1,0:T(8,128)(2,1)S(1)}, bf16[256,256]{1,0:T(8,128)(2,1)S(1)}, u32[]{:S(2)}, u32[]{:S(2)}) collective-permute-start(bf16[256,256]{1,0:T(8,128)(2,1)S(1)} %get-tuple-element.25), channel_id=1, source_target_pairs={{32,1},{1,32},{33,2},{2,33},{34,3},{3,34},{35,4},{4,35},{36,5},{5,... | collective-permute-start | bytes 393224 | tf_op jit(solution)/shard_map/ppermute | solution.py:459
  31.9 8.0 %collective-permute-start.6 = (bf16[256,256]{1,0:T(8,128)(2,1)S(1)}, bf16[256,256]{1,0:T(8,128)(2,1)S(1)}, u32[]{:S(2)}, u32[]{:S(2)}) collective-permute-start(bf16[256,256]{1,0:T(8,128)(2,1)S(1)} %get-tuple-element.24.x_own), channel_id=1, source_target_pairs={{32,33},{1,0},{33,34},{2,1},{34,35},{3,2},{35,36},{4,3},{36,37},{5... | collective-permute-start | bytes 393224 | tf_op jit(solution)/shard_map/ppermute | solution.py:458
  41.0 29.0 %collective-permute-start.9 = (bf16[256,256]{1,0:T(8,128)(2,1)S(1)}, bf16[256,256]{1,0:T(8,128)(2,1)S(1)}, u32[]{:S(2)}, u32[]{:S(2)}) collective-permute-start(bf16[256,256]{1,0:T(8,128)(2,1)S(1)} %get-tuple-element.30.refs_4_), channel_id=1, source_target_pairs={{1,0},{2,1},{3,2},{4,3},{5,4},{6,5},{7,6},{8,7},{9,8},{10,9},{11,1... | collective-permute-start | bytes 393224 | tf_op jit(solution)/shard_map/ppermute | solution.py:495
  42.3 27.7 %collective-permute-start.8 = (bf16[256,256]{1,0:T(8,128)(2,1)S(1)}, bf16[256,256]{1,0:T(8,128)(2,1)S(1)}, u32[]{:S(2)}, u32[]{:S(2)}) collective-permute-start(bf16[256,256]{1,0:T(8,128)(2,1)S(1)} %get-tuple-element.31.refs_5_), channel_id=1, source_target_pairs={{0,1},{1,2},{2,3},{3,4},{4,5},{5,6},{6,7},{7,8},{8,9},{9,10},{10,1... | collective-permute-start | bytes 393224 | tf_op jit(solution)/shard_map/ppermute | solution.py:496

commit v2 on v1

v2 whole, which is shorter than its diff:
```python
import functools

import jax
import jax.numpy as jnp
from jax import lax
from jax.experimental import pallas as pl
from jax.experimental.pallas import tpu as pltpu
from jax.sharding import PartitionSpec as P

F32 = jnp.float32
BF16 = jnp.bfloat16
AXES = ("seg", "sec")
QUARTER = 4
MIB = 1 << 20


def dot(first, second):
    return lax.dot_general(
        first, second, (((1,), (0,)), ((), ())), preferred_element_type=F32
    )


def vmem(count):
    return [pl.BlockSpec(memory_space=pltpu.VMEM)] * count


def smem(count):
    return [pl.BlockSpec(memory_space=pltpu.SMEM)] * count


def anywhere(count):
    return [pl.BlockSpec(memory_space=pl.ANY)] * count


def cost(products, size, bytes_accessed):
    return pl.CostEstimate(
        flops=2 * products * size**3, bytes_accessed=bytes_accessed, transcendentals=0
    )


def place():
    return lax.axis_index("seg") % 2


def limit(mebibytes):
    return pltpu.CompilerParams(vmem_limit_bytes=mebibytes * MIB)


def live(dim, size):
    rows = lax.broadcasted_iota(jnp.int32, (size, size), 0) < dim
    columns = lax.broadcasted_iota(jnp.int32, (size, size), 1) < dim
    return rows & columns


def in_hbm(array):
    return pltpu.with_memory_space_constraint(array, pltpu.HBM)


def split_kernel(gauge, state, own, other, gauge_here, state_here, sems):
    core = place()
    arrivals = [
        pltpu.make_async_copy(gauge, gauge_here, sems.at[0]),
        pltpu.make_async_copy(state, state_here, sems.at[1]),
    ]
    for copy in arrivals:
        copy.start()
    for copy in arrivals:
        copy.wait()
    own[0] = gauge_here[core].astype(BF16)
    own[1] = state_here[core]
    other[0] = gauge_here[1 - core].astype(BF16)
    other[1] = state_here[1 - core]


def table_kernel(charge_far, mask_far, dims_far, cells, table, charge, mask, dims, sems):
    channels, size = charge.shape[0], cells.shape[1]
    arrivals = [
        pltpu.make_async_copy(charge_far, charge, sems.at[0]),
        pltpu.make_async_copy(mask_far, mask, sems.at[1]),
        pltpu.make_async_copy(dims_far, dims, sems.at[2]),
    ]
    for copy in arrivals:
        copy.start()
    for copy in arrivals:
        copy.wait()
    ups, downs, rest = jnp.int32(0), jnp.int32(0), jnp.int32(0)
    for w in range(channels):
        up, down = charge[w] == 1, charge[w] == -1
        middle = QUARTER + rest
        table[0, jnp.where(up, ups, jnp.where(down, channels - QUARTER + downs, middle))] = w
        table[1, jnp.where(down, downs, jnp.where(up, channels - QUARTER + ups, middle))] = w
        ups = ups + up.astype(jnp.int32)
        downs = downs + down.astype(jnp.int32)
        rest = rest + jnp.where(up | down, 0, 1)
    for s in range(2):
        for j in range(channels):
            table[2 + s, j] = mask[s, table[s, j]]
        cells[s] = jnp.where(live(dims[s], size), 1.0, 0.0).astype(BF16)


def sort_kernel(table, left, right, left_sorted, right_sorted, sems):
    channels = left.shape[1]

    def copy(side, s, j):
        source, target = ((left, left_sorted), (right, right_sorted))[side]
        return pltpu.make_async_copy(
            source.at[s, table[s, j]], target.at[s, j], sems.at[side, s, j]
        )

    every = [(side, s, j) for side in range(2) for s in range(2) for j in range(channels)]
    for where in every:
        copy(*where).start()
    for where in every:
        copy(*where).wait()
    for s in range(2):
        for j in range(channels):
            @pl.when(table[2 + s, j] == 0)
            def _():
                right_sorted[s, j] = jnp.zeros(right_sorted.shape[2:], right_sorted.dtype)


def relay_kernel(pair, after, out):
    out[...] = pair[1]


def joined(later, earlier):
    return later.astype(F32) + earlier.astype(F32) + dot(later, earlier)


def pair_kernel(own, got, after, out):
    core = place()

    @pl.when(core == 0)
    def _():
        out[...] = joined(got[0], own[0]).astype(BF16)

    @pl.when(core == 1)
    def _():
        out[...] = joined(own[0], got[0]).astype(BF16)


def state_kernel(cells, own, got, one_back, two_back, three_back, *refs):
    x_pair, pair = refs[-2:]
    core = place()
    size = x_pair.shape[1]
    pair[core] = own[...]
    pair[1 - core] = got[...]
    field = jnp.concatenate([pair[0, 1], pair[1, 1]], axis=1)
    wide = field.astype(F32)
    wide = wide + dot(three_back[...], field)
    wide = wide + dot(two_back[...], wide.astype(BF16))
    wide = wide + dot(one_back[...], wide.astype(BF16))
    wide = wide + dot(pair[0, 0], wide.astype(BF16))
    earlier, later = wide[:, :size], wide[:, size:]
    later = later + dot(pair[1, 0], later.astype(BF16))
    alive = cells[core] != 0
    first = jnp.where(alive, earlier, 0.0).astype(BF16)
    second = jnp.where(alive, later, 0.0).astype(BF16)
    x_pair[core] = first
    x_pair[1 - core] = second


def spread(parts, s, blocks, field, first, last):
    size = field.shape[0]
    rows = blocks[s, first:last].reshape((last - first) * size, size)
    result = dot(rows, field).astype(BF16)
    for j in range(first, last):
        at = (j - first) * size
        parts[s, :, j * size : (j + 1) * size] = result[at : at + size]


def folded(parts, s, blocks, first, last):
    size = blocks.shape[-1]
    rows = blocks[s, first:last].reshape((last - first) * size, size)
    return dot(parts[s, :, first * size : last * size], rows)


def own_kernel(x_pair, x_swapped, left, right, table_far, acc, env, x_here, crossing, parts,
               blocks, table, table_sem, out_sems):
    core = place()
    channels, size = left.shape[1], left.shape[2]
    cross = channels - QUARTER
    fetch = pltpu.make_async_copy(table_far, table, table_sem.at[0])
    fetch.start()
    x_here[core] = x_pair[0]
    x_here[1 - core] = x_swapped[1]

    def send(s, j):
        target = 1 - s if j < QUARTER else s
        return pltpu.make_async_copy(
            blocks.at[s, j], env.at[0, target, table[s, j]], out_sems.at[s, j]
        )

    for s in range(2):
        field = x_here[s]
        turned = field.T
        spread(parts, s, left, field, 0, channels)
        result = dot(turned, parts[s]).astype(BF16)
        for j in range(cross):
            blocks[s, j] = result[:, j * size : (j + 1) * size]
        for j in range(cross, channels):
            crossing[s, j - cross] = result[:, j * size : (j + 1) * size]
        if s == 0:
            fetch.wait()
        for j in range(cross):
            send(s, j).start()
    for s in range(2):
        spread(parts, s, left, x_here[1 - s], cross, channels)
        acc[s] = folded(parts, s, right, QUARTER, channels)
    for s in range(2):
        for j in range(cross):
            send(s, j).wait()


def image_kernel(cells, x_here, side_same, side_swapped, left, right, acc, crossing, to_left,
                 to_right, sums, x_side, parts):
    core = place()
    x_side[1 - core] = side_same[0]
    x_side[core] = side_swapped[...]
    total = []
    for s in range(2):
        spread(parts, s, left, x_side[s], 0, QUARTER)
        image = acc[s] + folded(parts, s, right, 0, QUARTER)
        image = jnp.where(cells[s] != 0, image, 0.0).astype(BF16)
        message = (to_left, to_right)[s]
        message[:QUARTER] = crossing[s]
        message[QUARTER] = image
        total.append(image)

    def whole(values):
        return jnp.sum(jnp.sum(values, axis=0, keepdims=True), axis=1, keepdims=True)

    x_wide = [x_here[s].astype(F32) for s in range(2)]
    v_wide = [total[s].astype(F32) for s in range(2)]
    norm = whole(x_wide[0] * x_wide[0] + x_wide[1] * x_wide[1])
    correlation = whole(x_wide[0] * v_wide[0] + x_wide[1] * v_wide[1])
    ratio = jnp.where(norm > 0.0, correlation / jnp.where(norm > 0.0, norm, 1.0), 0.0)
    apart = [v_wide[s] - ratio * x_wide[s] for s in range(2)]
    spread_of = whole(apart[0] * apart[0] + apart[1] * apart[1])
    lane = lax.broadcasted_iota(jnp.int32, sums.shape, 1)
    row = jnp.where(lane == 0, norm, jnp.where(lane == 1, correlation, 0.0))
    row = jnp.where(lane == 2, ratio, jnp.where(lane == 3, spread_of, row))
    sums[...] = row


def apart_kernel(sums, x_here, to_left, to_right, left, right, image, sums_out, parts):
    channels = left.shape[1]
    cross = channels - QUARTER
    ratio = sums[0:1, 2:3]

    def apart(v, x):
        return (v.astype(F32) - ratio * x.astype(F32)).astype(BF16)

    inner = [apart((to_left, to_right)[s][QUARTER], x_here[s]) for s in range(2)]
    for s in range(2):
        spread(parts, s, left, inner[s], QUARTER, cross)
        spread(parts, s, left, inner[1 - s], cross, channels)
        image[s] = folded(parts, s, right, QUARTER, channels)
    sums_out[...] = sums[...]


def krylov_kernel(total_cells, cells, sums, sums_here, image, acc, x_side, from_left, from_right,
                  left, right, table_far, env_in, krylov, env, rayleigh, parts, table,
                  table_sem, out_sems):
    fetch = pltpu.make_async_copy(table_far, table, table_sem.at[0])
    fetch.start()
    column = [jnp.sum(sums[:, i : i + 1], axis=0, keepdims=True) for i in range(2)]
    ratio = column[1] / column[0]
    apart = ratio - sums[:, 2:3]
    spread_of = jnp.sum(sums[:, 3:4] + apart * apart * sums[:, 0:1], axis=0, keepdims=True)
    inverse = 1.0 / jnp.sqrt(spread_of * (1.0 / total_cells) + 1e-06)
    rayleigh[0] = ratio[0, 0]
    missing = ratio - sums_here[0:1, 2:3]

    def send(s, j):
        return pltpu.make_async_copy(
            (from_left, from_right)[s].at[j], env.at[0, s, table[s, j]], out_sems.at[s, j]
        )

    for s in range(2):
        arrived = (from_left, from_right)[s][QUARTER].astype(F32)
        outer = (arrived - ratio * x_side[s].astype(F32)).astype(BF16)
        spread(parts, s, left, outer, 0, QUARTER)
        if s == 0:
            fetch.wait()
            for t in range(2):
                for j in range(QUARTER):
                    send(t, j).start()
        whole = image[s] - missing * acc[s] + folded(parts, s, right, 0, QUARTER)
        krylov[0, s] = jnp.where(cells[s] != 0, whole * inverse, 0.0).astype(BF16)
    for s in range(2):
        for j in range(QUARTER):
            send(s, j).wait()


def local(state_blocks, gauge_offset, left_env, right_env, mpo_mask, charge, block_dims):
    size = state_blocks.shape[-1]
    channels = left_env.shape[2]
    segments = lax.axis_size("seg")
    groups = lax.axis_size("sec")
    block = (size, size)

    def at(segment, group):
        return segment * groups + group

    every = range(groups)
    swap = [(at(k, i), at(k ^ 1, i)) for k in range(segments) for i in every]
    def onward(chips):
        return [
            (at(k, i), at(k + 2 * chips, i)) for k in range(segments - 2 * chips) for i in every
        ]

    same = [
        (at(2 * c + r, i), at(2 * c + r, i + 2 * r - 1))
        for c in range(segments // 2) for r in range(2) for i in every
        if 0 <= i + 2 * r - 1 < groups
    ]
    leftward = [(i, i - 1) for i in range(1, groups)]
    rightward = [(i, i + 1) for i in range(groups - 1)]

    left, right = in_hbm(left_env[0]), in_hbm(right_env[0])
    whole = (2, channels) + block
    own, other = pl.pallas_call(
        split_kernel,
        out_shape=[jax.ShapeDtypeStruct((2,) + block, BF16)] * 2,
        in_specs=anywhere(2),
        out_specs=vmem(2),
        scratch_shapes=[
            pltpu.VMEM((2,) + block, F32),
            pltpu.VMEM((2,) + block, BF16),
            pltpu.SemaphoreType.DMA((2,)),
        ],
        compiler_params=limit(4),
        cost_estimate=cost(0, size, 2 * MIB),
    )(in_hbm(gauge_offset[0]), in_hbm(state_blocks[0]))
    got = lax.ppermute(other, AXES, swap)
    cells, table = pl.pallas_call(
        table_kernel,
        out_shape=[
            jax.ShapeDtypeStruct((2,) + block, BF16),
            jax.ShapeDtypeStruct((4, channels), jnp.int32),
        ],
        in_specs=anywhere(3),
        out_specs=vmem(1) + smem(1),
        scratch_shapes=[
            pltpu.SMEM(charge.shape, jnp.int32),
            pltpu.SMEM(mpo_mask.shape, jnp.int32),
            pltpu.SMEM(block_dims.shape, jnp.int32),
            pltpu.SemaphoreType.DMA((3,)),
        ],
        compiler_params=limit(4),
        cost_estimate=cost(0, size, 2 * MIB),
    )(in_hbm(charge), in_hbm(mpo_mask), in_hbm(block_dims))

    pair = pl.pallas_call(
        pair_kernel,
        out_shape=jax.ShapeDtypeStruct(block, BF16),
        in_specs=vmem(2) + anywhere(1),
        out_specs=vmem(1)[0],
        compiler_params=limit(4),
        cost_estimate=cost(1, size, MIB),
    )(own, got, cells)
    backs = [lax.ppermute(pair, AXES, onward(chips)) for chips in range(1, segments // 2)]
    left_sorted, right_sorted = pl.pallas_call(
        sort_kernel,
        out_shape=[jax.ShapeDtypeStruct(whole, BF16)] * 2,
        in_specs=smem(1) + anywhere(2),
        out_specs=vmem(2),
        scratch_shapes=[pltpu.SemaphoreType.DMA((2, 2, channels))],
        compiler_params=limit(4),
        cost_estimate=cost(0, size, 16 * MIB),
    )(table, left, right)
    x_pair = pl.pallas_call(
        state_kernel,
        out_shape=jax.ShapeDtypeStruct((2,) + block, BF16),
        in_specs=vmem(6) + anywhere(1),
        out_specs=vmem(1)[0],
        scratch_shapes=[pltpu.VMEM((2, 2) + block, BF16)],
        compiler_params=limit(6),
        cost_estimate=cost(8, size, 2 * MIB),
    )(cells, own, got, *backs, right_sorted)
    x_swapped = lax.ppermute(x_pair, AXES, swap)
    side_same = lax.ppermute(x_pair, AXES, same)
    acc, env, x_here, crossing = pl.pallas_call(
        own_kernel,
        out_shape=[
            jax.ShapeDtypeStruct((2,) + block, F32),
            pltpu.HBM((1, 2, channels) + block, BF16),
            jax.ShapeDtypeStruct((2,) + block, BF16),
            jax.ShapeDtypeStruct((2, QUARTER) + block, BF16),
        ],
        in_specs=vmem(4) + anywhere(1),
        out_specs=vmem(1) + anywhere(1) + vmem(2),
        scratch_shapes=[
            pltpu.VMEM((2, size, channels * size), BF16),
            pltpu.VMEM((2, channels - QUARTER) + block, BF16),
            pltpu.SMEM((4, channels), jnp.int32),
            pltpu.SemaphoreType.DMA((1,)),
            pltpu.SemaphoreType.DMA((2, channels - QUARTER)),
        ],
        compiler_params=limit(12),
        cost_estimate=cost(96, size, 12 * MIB),
    )(x_pair, x_swapped, left_sorted, right_sorted, table)

    relayed = pl.pallas_call(
        relay_kernel,
        out_shape=jax.ShapeDtypeStruct(block, BF16),
        in_specs=vmem(1) + anywhere(1),
        out_specs=vmem(1)[0],
        compiler_params=limit(2),
        cost_estimate=cost(0, size, MIB),
    )(side_same, acc)
    side_swapped = lax.ppermute(relayed, AXES, swap)
    to_left, to_right, sums, x_side = pl.pallas_call(
        image_kernel,
        out_shape=[
            jax.ShapeDtypeStruct((QUARTER + 1,) + block, BF16),
            jax.ShapeDtypeStruct((QUARTER + 1,) + block, BF16),
            pltpu.VMEM((groups, 128), F32),
            jax.ShapeDtypeStruct((2,) + block, BF16),
        ],
        in_specs=vmem(8),
        out_specs=vmem(4),
        scratch_shapes=[pltpu.VMEM((2, size, QUARTER * size), BF16)],
        compiler_params=limit(10),
        cost_estimate=cost(16, size, 4 * MIB),
    )(cells, x_here, side_same, side_swapped, left_sorted, right_sorted, acc, crossing)
    from_right = lax.ppermute(to_left, "sec", leftward)
    from_left = lax.ppermute(to_right, "sec", rightward)
    image, sums_here = pl.pallas_call(
        apart_kernel,
        out_shape=[
            jax.ShapeDtypeStruct((2,) + block, F32),
            pltpu.VMEM((groups, 128), F32),
        ],
        in_specs=vmem(6),
        out_specs=vmem(2),
        scratch_shapes=[pltpu.VMEM((2, size, channels * size), BF16)],
        compiler_params=limit(10),
        cost_estimate=cost(48, size, 4 * MIB),
    )(sums, x_here, to_left, to_right, left_sorted, right_sorted)
    sums = lax.all_to_all(sums_here, "sec", 0, 0)

    total_cells = float(groups * 2 * size * size)
    krylov, env, rayleigh = pl.pallas_call(
        functools.partial(krylov_kernel, total_cells),
        out_shape=[
            jax.ShapeDtypeStruct((1, 2) + block, BF16),
            jax.ShapeDtypeStruct((1, 2, channels) + block, BF16),
            jax.ShapeDtypeStruct((1,), F32),
        ],
        in_specs=vmem(10) + anywhere(2),
        out_specs=vmem(1) + anywhere(1) + smem(1),
        scratch_shapes=[
            pltpu.VMEM((2, size, QUARTER * size), BF16),
            pltpu.SMEM((4, channels), jnp.int32),
            pltpu.SemaphoreType.DMA((1,)),
            pltpu.SemaphoreType.DMA((2, QUARTER)),
        ],
        input_output_aliases={11: 1},
        compiler_params=limit(8),
        cost_estimate=cost(16, size, 4 * MIB),
    )(cells, sums, sums_here, image, acc, x_side, from_left, from_right, left_sorted,
      right_sorted, table, env)
    return krylov, env, rayleigh


def solution(mesh):
    return jax.shard_map(
        local,
        mesh=mesh,
        in_specs=(
            P("seg", "sec", None, None),
            P("seg", "sec", None, None),
            P("seg", "sec", None, None, None),
            P("seg", "sec", None, None, None),
            P("sec", None),
            P(),
            P("sec"),
        ),
        out_specs=(P("seg", "sec", None, None), P("seg", "sec", None, None, None), P("seg")),
        check_vma=False,
    )
```

time: 79.7 us -> 66.6 us (0.84)
  starting transfers between devices: 27.6 us -> 19.2 us
  Pallas kernels: 26 us -> 20.3 us
  waiting for transfers between devices: 0.4 us -> 1.36 us
  blocking collectives: 23.7 us -> 24.6 us
    ppermute x9 -> x8, starting transfers between devices: 24.3 us -> 15.9 us  [the longest x3 6.69 us: local(): lax.ppermute(pair, AXES, onward(chips))]
    pallas_call x6, Pallas kernels: 16.9 us -> 12 us  [the longest x1 4.85 us: local(): pl.pallas_call(sort_kernel, out_shape=[jax.ShapeDtypeStruct(whole, BF16)]...]
    pallas_call x1, Pallas kernels: 2.86 us -> 1.55 us  [local(): pl.pallas_call(table_kernel, out_shape=[jax.ShapeDtypeStruct((2,) + block...]
    all_to_all x1, blocking collectives: 23.7 us -> 24.6 us  [local(): sums = lax.all_to_all(sums_here, 'sec', 0, 0)]
    ppermute x9 -> x8, waiting for transfers between devices: 0.4 us -> 1.35 us  [the longest x1 1.33 us: local(): side_swapped = lax.ppermute(relayed, AXES, swap)]
  transfers between devices with their start and end apart: 10 -> 9, of which waited for: 1 -> 1; matrix products, arithmetic and copies ran while one was open for 0% -> 0% of each run, Pallas kernels for 18% -> 21%
where the time goes in v2:
time: 66.6 us; the launch traced here: 66.3 us
  blocking collectives  24.6 us (37%)
  Pallas kernels  20.3 us (30%)
  starting transfers between devices  19.2 us (29%)
  waiting for transfers between devices  1.36 us (2%)
  between operations  0.79 us (1%)
    all_to_all x1, blocking collectives, local(): sums = lax.all_to_all(sums_here, 'sec', 0, 0)  24.6 us
    ppermute x3, starting transfers between devices, local(): lax.ppermute(pair, AXES, onward(chips))  6.69 us
    pallas_call x1, Pallas kernels, local(): pl.pallas_call(own_kernel, out_shape=[jax.ShapeDtypeStruct((2,) + block,...  5.38 us
    pallas_call x1, Pallas kernels, local(): pl.pallas_call(sort_kernel, out_shape=[jax.ShapeDtypeStruct(whole, BF16)]...  4.85 us
    ppermute x1, starting transfers between devices, local(): from_left = lax.ppermute(to_right, 'sec', rightward)  4.03 us
    ppermute x1, starting transfers between devices, local(): got = lax.ppermute(other, AXES, swap)  3.33 us
    ppermute x1, starting transfers between devices, local(): side_same = lax.ppermute(x_pair, AXES, same)  3.11 us
    pallas_call x1, Pallas kernels, local(): pl.pallas_call(functools.partial(krylov_kernel, total_cells), out_shape=[...  2.92 us
  transfers between devices with their start and end apart: 9, of which 1 were waited for; matrix products, arithmetic and copies ran while one was open for 0% of the time, Pallas kernels for 21%

profile of v2, /device:TPU:1, one launch (start us, length us, event | category | flops | bytes accessed | tf_op | source)
XLA Modules:
  0.0 66.3 jit_solution(9476797882798026774)
XLA Ops:
  0.6 1.2 %shard_map.95 = (bf16[2,256,256]{2,1,0:T(8,128)(2,1)S(1)}, bf16[2,256,256]{2,1,0:T(8,128)(2,1)S(1)}) custom-call(f32[2,256,256]{2,1,0:T(8,128)} %bitcast.12, bf16[2,256,256]{2,1,0:T(8,128)(2,1)} %bitcast.13), custom_call_target="tpu_custom_call" | custom-call | bytes 2097152 | tf_op jit(solution)/shard_map/pallas_call | solution.py:323
  1.8 3.3 %collective-permute-start = (bf16[2,256,256]{2,1,0:T(8,128)(2,1)S(1)}, bf16[2,256,256]{2,1,0:T(8,128)(2,1)S(1)}, u32[]{:S(2)}, u32[]{:S(2)}) collective-permute-start(bf16[2,256,256]{2,1,0:T(8,128)(2,1)S(1)} %get-tuple-element.21), channel_id=1, source_target_pairs={{0,32},{1,33},{2,34},{3,35},{4,36},{5,37},{6,38},{7,39},{8,40},{9,... | collective-permute-start | bytes 786440 | tf_op jit(solution)/shard_map/ppermute | solution.py:336
  5.1 1.6 %shard_map.94 = (bf16[2,256,256]{2,1,0:T(8,128)(2,1)S(1)}, s32[4,16]{1,0:T(4,128)S(1)}) custom-call(s32[16]{0:T(128)} %charge_far.1, s32[2,16]{1,0:T(2,128)} %mask_far.1, s32[2]{0:T(128)} %dims_far.1), custom_call_target="tpu_custom_call" | custom-call | bytes 2097152 | tf_op jit(solution)/shard_map/pallas_call | solution.py:337
  6.7 0.0 collective-permute-done.got
  6.7 0.2 shard_map.96
  6.9 2.9 %collective-permute-start.3 = (bf16[256,256]{1,0:T(8,128)(2,1)S(1)}, bf16[256,256]{1,0:T(8,128)(2,1)S(1)}, u32[]{:S(2)}, u32[]{:S(2)}) collective-permute-start(bf16[256,256]{1,0:T(8,128)(2,1)S(1)} %shard_map.96), channel_id=1, source_target_pairs={{0,192},{1,193},{2,194},{3,195},{4,196},{5,197},{6,198},{7,199},{8... | collective-permute-start | bytes 393224 | tf_op jit(solution)/shard_map/ppermute | solution.py:363
  9.8 1.3 %collective-permute-start.2 = (bf16[256,256]{1,0:T(8,128)(2,1)S(1)}, bf16[256,256]{1,0:T(8,128)(2,1)S(1)}, u32[]{:S(2)}, u32[]{:S(2)}) collective-permute-start(bf16[256,256]{1,0:T(8,128)(2,1)S(1)} %shard_map.96), channel_id=1, source_target_pairs={{0,128},{1,129},{2,130},{3,131},{4,132},{5,133},{6,134},{7,135},{8... | collective-permute-start | bytes 393224 | tf_op jit(solution)/shard_map/ppermute | solution.py:363
  11.1 2.5 %collective-permute-start.1 = (bf16[256,256]{1,0:T(8,128)(2,1)S(1)}, bf16[256,256]{1,0:T(8,128)(2,1)S(1)}, u32[]{:S(2)}, u32[]{:S(2)}) collective-permute-start(bf16[256,256]{1,0:T(8,128)(2,1)S(1)} %shard_map.96), channel_id=1, source_target_pairs={{0,64},{1,65},{2,66},{3,67},{4,68},{5,69},{6,70},{7,71},{8,72},{9,... | collective-permute-start | bytes 393224 | tf_op jit(solution)/shard_map/ppermute | solution.py:363
  13.6 4.9 %shard_map.97 = (bf16[2,16,256,256]{3,2,1,0:T(8,128)(2,1)S(1)}, bf16[2,16,256,256]{3,2,1,0:T(8,128)(2,1)S(1)}) custom-call(s32[4,16]{1,0:T(4,128)S(1)} %get-tuple-element.22.table.table_far, bf16[2,16,256,256]{3,2,1,0:T(8,128)(2,1)} %bitcast.10, bf16[2,16,256,256]{3,2,1,0:T(8,128)(2,1)} %bitcast.11), custom_call_target="tpu_custom_call" | custom-call | bytes 16777216 | tf_op jit(solution)/shard_map/pallas_call | solution.py:364
  18.5 0.0 collective-permute-done.3.three_back
  18.5 0.0 collective-permute-done.2.two_back
  18.5 0.0 collective-permute-done.1.one_back
  18.5 1.0 %shard_map.98.x_pair = bf16[2,256,256]{2,1,0:T(8,128)(2,1)S(1)} custom-call(bf16[2,256,256]{2,1,0:T(8,128)(2,1)S(1)} %get-tuple-element.19.after.cells, bf16[2,256,256]{2,1,0:T(8,128)(2,1)S(1)} %get-tuple-element.20.own, bf16[2,256,256]{2,1,0:T(8,128)(2,1)S(1)} %collective-permute-done.got, bf16[256,256]{1,0:T(8,128)(2,1)S(1)} %collective-permute-done.1.one_back, ...), custom_call_target="tpu_custom_call" | custom-call | flops 268435456 | bytes 2097152 | tf_op jit(solution)/shard_map/pallas_call | solution.py:373
  19.6 0.7 %collective-permute-start.4 = (bf16[2,256,256]{2,1,0:T(8,128)(2,1)S(1)}, bf16[2,256,256]{2,1,0:T(8,128)(2,1)S(1)}, u32[]{:S(2)}, u32[]{:S(2)}) collective-permute-start(bf16[2,256,256]{2,1,0:T(8,128)(2,1)S(1)} %shard_map.98.x_pair), channel_id=1, source_target_pairs={{0,32},{1,33},{2,34},{3,35},{4,36},{5,37},{6,38},{7,39},{8,40},{9,... | collective-permute-start | bytes 786440 | tf_op jit(solution)/shard_map/ppermute | solution.py:382
  20.2 3.1 %collective-permute-start.5 = (bf16[2,256,256]{2,1,0:T(8,128)(2,1)S(1)}, bf16[2,256,256]{2,1,0:T(8,128)(2,1)S(1)}, u32[]{:S(2)}, u32[]{:S(2)}) collective-permute-start(bf16[2,256,256]{2,1,0:T(8,128)(2,1)S(1)} %shard_map.98.x_pair), channel_id=1, source_target_pairs={{1,0},{2,1},{3,2},{4,3},{5,4},{6,5},{7,6},{8,7},{9,8},{10,9},{11,1... | collective-permute-start | bytes 786440 | tf_op jit(solution)/shard_map/ppermute | solution.py:383
  23.4 0.0 collective-permute-done.4.x_swapped
  23.4 5.4 %shard_map.99 = (f32[2,256,256]{2,1,0:T(8,128)S(1)}, bf16[1,2,16,256,256]{4,3,2,1,0:T(8,128)(2,1)}, bf16[2,256,256]{2,1,0:T(8,128)(2,1)S(1)}, bf16[2,4,256,256]{3,2,1,0:T(8,128)(2,1)S(1)}) custom-call(bf16[2,256,256]{2,1,0:T(8,128)(2,1)S(1)} %shard_map.98.x_pair, bf16[2,256,256]{2,1,0:T(8,128)(2,1)S(1)} %collective-permute-done.4.x_swapped, ...), custom_call_target="tpu_custom_call" | custom-call | flops 3221225472 | bytes 12582912 | tf_op jit(solution)/shard_map/pallas_call | solution.py:384
  28.8 0.0 collective-permute-done.5.pair.side_same
  28.8 0.1 collective-permute-start.6
  28.9 1.3 %collective-permute-done.6.side_swapped = bf16[256,256]{1,0:T(8,128)(2,1)S(1)} collective-permute-done((bf16[256,256]{1,0:T(8,128)(2,1)S(1)}, bf16[256,256]{1,0:T(8,128)(2,1)S(1)}, u32[]{:S(2)}, u32[]{:S(2)}) %collective-permute-start.6) | collective-permute-done | bytes 131104 | tf_op jit(solution)/shard_map/ppermute | solution.py:413
  30.2 1.2 %shard_map.101 = (bf16[5,256,256]{2,1,0:T(8,128)(2,1)S(1)}, bf16[5,256,256]{2,1,0:T(8,128)(2,1)S(1)}, f32[32,128]{1,0:T(8,128)S(1)}, bf16[2,256,256]{2,1,0:T(8,128)(2,1)S(1)}) custom-call(bf16[2,256,256]{2,1,0:T(8,128)(2,1)S(1)} %get-tuple-element.19.after.cells, bf16[2,256,256]{2,1,0:T(8,128)(2,1)S(1)} %get-tuple-element.25.x_here, ...), custom_call_target="tpu_custom_call" | custom-call | flops 536870912 | bytes 4194304 | tf_op jit(solution)/shard_map/pallas_call | solution.py:414
  31.4 1.3 %collective-permute-start.8 = (bf16[5,256,256]{2,1,0:T(8,128)(2,1)S(1)}, bf16[5,256,256]{2,1,0:T(8,128)(2,1)S(1)}, u32[]{:S(2)}, u32[]{:S(2)}) collective-permute-start(bf16[5,256,256]{2,1,0:T(8,128)(2,1)S(1)} %get-tuple-element.29.to_left), channel_id=1, source_target_pairs={{1,0},{2,1},{3,2},{4,3},{5,4},{6,5},{7,6},{8,7},{9,8},{10,9},{11,1... | collective-permute-start | bytes 1966088 | tf_op jit(solution)/shard_map/ppermute | solution.py:428
  32.7 4.0 %collective-permute-start.7 = (bf16[5,256,256]{2,1,0:T(8,128)(2,1)S(1)}, bf16[5,256,256]{2,1,0:T(8,128)(2,1)S(1)}, u32[]{:S(2)}, u32[]{:S(2)}) collective-permute-start(bf16[5,256,256]{2,1,0:T(8,128)(2,1)S(1)} %get-tuple-element.30.to_right), channel_id=1, source_target_pairs={{0,1},{1,2},{2,3},{3,4},{4,5},{5,6},{6,7},{7,8},{8,9},{9,10},{10,1... | collective-permute-start | bytes 1966088 | tf_op jit(solution)/shard_map/ppermute | solution.py:429
  36.7 2.0 %shard_map.102 = (f32[2,256,256]{2,1,0:T(8,128)S(1)}, f32[32,128]{1,0:T(8,128)S(1)}) custom-call(f32[32,128]{1,0:T(8,128)S(1)} %get-tuple-element.28.sums, bf16[2,256,256]{2,1,0:T(8,128)(2,1)S(1)} %get-tuple-element.25.x_here, bf16[5,256,256]{2,1,0:T(8,128)(2,1)S(1)} %get-tuple-element.29.to_left, bf16[5,256,256]{2,1,0:T(8,128)(2,1)S(1)} %get-tuple-element.30.to_right, ...), custom_call_target="tpu_custom_call" | custom-call | flops 1610612736 | bytes 4194304 | tf_op jit(solution)/shard_map/pallas_call | solution.py:430
  38.8 24.6 %all_to_all.11 = f32[32,1,128]{2,1,0:T(1,128)S(1)} all-to-all(f32[32,1,128]{2,1,0:T(1,128)S(1)} %bitcast.8), channel_id=1, replica_groups=mesh['seg'=8,'sec'=32] {'sec'}, dimensions={0} | all-to-all | bytes 32768 | tf_op jit(solution)/shard_map/all_to_all | solution.py:442
  63.4 0.0 collective-permute-done.8.from_right
  63.4 0.0 collective-permute-done.7.from_left
  63.4 2.9 %shard_map.103 = (bf16[1,2,256,256]{3,2,1,0:T(8,128)(2,1)}, bf16[1,2,16,256,256]{4,3,2,1,0:T(8,128)(2,1)}, f32[1]{0:T(128)}) custom-call(bf16[2,256,256]{2,1,0:T(8,128)(2,1)S(1)} %get-tuple-element.19.after.cells, f32[32,128]{1,0:T(8,128)S(1)} %bitcast.9, f32[32,128]{1,0:T(8,128)S(1)} %get-tuple-element.31.sums_here, ...), custom_call_target="tpu_custom_call", output_to_operand_aliasing={{1}: (11, {})} | custom-call | flops 536870912 | bytes 4194304 | tf_op jit(solution)/shard_map/pallas_call | solution.py:445
  (1 shorter events, 0.0 us)
Async XLA Ops:
  1.8 4.9 %collective-permute-start = (bf16[2,256,256]{2,1,0:T(8,128)(2,1)S(1)}, bf16[2,256,256]{2,1,0:T(8,128)(2,1)S(1)}, u32[]{:S(2)}, u32[]{:S(2)}) collective-permute-start(bf16[2,256,256]{2,1,0:T(8,128)(2,1)S(1)} %get-tuple-element.21), channel_id=1, source_target_pairs={{0,32},{1,33},{2,34},{3,35},{4,36},{5,37},{6,38},{7,39},{8,40},{9,... | collective-permute-start | bytes 786440 | tf_op jit(solution)/shard_map/ppermute | solution.py:336
  6.9 11.6 %collective-permute-start.3 = (bf16[256,256]{1,0:T(8,128)(2,1)S(1)}, bf16[256,256]{1,0:T(8,128)(2,1)S(1)}, u32[]{:S(2)}, u32[]{:S(2)}) collective-permute-start(bf16[256,256]{1,0:T(8,128)(2,1)S(1)} %shard_map.96), channel_id=1, source_target_pairs={{0,192},{1,193},{2,194},{3,195},{4,196},{5,197},{6,198},{7,199},{8... | collective-permute-start | bytes 393224 | tf_op jit(solution)/shard_map/ppermute | solution.py:363
  9.8 8.7 %collective-permute-start.2 = (bf16[256,256]{1,0:T(8,128)(2,1)S(1)}, bf16[256,256]{1,0:T(8,128)(2,1)S(1)}, u32[]{:S(2)}, u32[]{:S(2)}) collective-permute-start(bf16[256,256]{1,0:T(8,128)(2,1)S(1)} %shard_map.96), channel_id=1, source_target_pairs={{0,128},{1,129},{2,130},{3,131},{4,132},{5,133},{6,134},{7,135},{8... | collective-permute-start | bytes 393224 | tf_op jit(solution)/shard_map/ppermute | solution.py:363
  11.1 7.4 %collective-permute-start.1 = (bf16[256,256]{1,0:T(8,128)(2,1)S(1)}, bf16[256,256]{1,0:T(8,128)(2,1)S(1)}, u32[]{:S(2)}, u32[]{:S(2)}) collective-permute-start(bf16[256,256]{1,0:T(8,128)(2,1)S(1)} %shard_map.96), channel_id=1, source_target_pairs={{0,64},{1,65},{2,66},{3,67},{4,68},{5,69},{6,70},{7,71},{8,72},{9,... | collective-permute-start | bytes 393224 | tf_op jit(solution)/shard_map/ppermute | solution.py:363
  19.6 3.8 %collective-permute-start.4 = (bf16[2,256,256]{2,1,0:T(8,128)(2,1)S(1)}, bf16[2,256,256]{2,1,0:T(8,128)(2,1)S(1)}, u32[]{:S(2)}, u32[]{:S(2)}) collective-permute-start(bf16[2,256,256]{2,1,0:T(8,128)(2,1)S(1)} %shard_map.98.x_pair), channel_id=1, source_target_pairs={{0,32},{1,33},{2,34},{3,35},{4,36},{5,37},{6,38},{7,39},{8,40},{9,... | collective-permute-start | bytes 786440 | tf_op jit(solution)/shard_map/ppermute | solution.py:382
  20.2 8.5 %collective-permute-start.5 = (bf16[2,256,256]{2,1,0:T(8,128)(2,1)S(1)}, bf16[2,256,256]{2,1,0:T(8,128)(2,1)S(1)}, u32[]{:S(2)}, u32[]{:S(2)}) collective-permute-start(bf16[2,256,256]{2,1,0:T(8,128)(2,1)S(1)} %shard_map.98.x_pair), channel_id=1, source_target_pairs={{1,0},{2,1},{3,2},{4,3},{5,4},{6,5},{7,6},{8,7},{9,8},{10,9},{11,1... | collective-permute-start | bytes 786440 | tf_op jit(solution)/shard_map/ppermute | solution.py:383
  28.8 1.4 %collective-permute-start.6 = (bf16[256,256]{1,0:T(8,128)(2,1)S(1)}, bf16[256,256]{1,0:T(8,128)(2,1)S(1)}, u32[]{:S(2)}, u32[]{:S(2)}) collective-permute-start(bf16[256,256]{1,0:T(8,128)(2,1)S(1)} %shard_map.100), channel_id=1, source_target_pairs={{0,32},{1,33},{2,34},{3,35},{4,36},{5,37},{6,38},{7,39},{8,40},{9,... | collective-permute-start | bytes 393224 | tf_op jit(solution)/shard_map/ppermute | solution.py:413
  31.4 32.0 %collective-permute-start.8 = (bf16[5,256,256]{2,1,0:T(8,128)(2,1)S(1)}, bf16[5,256,256]{2,1,0:T(8,128)(2,1)S(1)}, u32[]{:S(2)}, u32[]{:S(2)}) collective-permute-start(bf16[5,256,256]{2,1,0:T(8,128)(2,1)S(1)} %get-tuple-element.29.to_left), channel_id=1, source_target_pairs={{1,0},{2,1},{3,2},{4,3},{5,4},{6,5},{7,6},{8,7},{9,8},{10,9},{11,1... | collective-permute-start | bytes 1966088 | tf_op jit(solution)/shard_map/ppermute | solution.py:428
  32.7 30.7 %collective-permute-start.7 = (bf16[5,256,256]{2,1,0:T(8,128)(2,1)S(1)}, bf16[5,256,256]{2,1,0:T(8,128)(2,1)S(1)}, u32[]{:S(2)}, u32[]{:S(2)}) collective-permute-start(bf16[5,256,256]{2,1,0:T(8,128)(2,1)S(1)} %get-tuple-element.30.to_right), channel_id=1, source_target_pairs={{0,1},{1,2},{2,3},{3,4},{4,5},{5,6},{6,7},{7,8},{8,9},{9,10},{10,1... | collective-permute-start | bytes 1966088 | tf_op jit(solution)/shard_map/ppermute | solution.py:429

commit v3 on v2

--- a/solution.py
+++ b/solution.py
@@ -40,6 +40,10 @@
 
 def place():
     return lax.axis_index("seg") % 2
+
+
+def odd_place():
+    return lax.axis_index("sec") % 2 == 1
 
 
 def limit(mebibytes):
@@ -120,7 +124,7 @@
 
 
 def relay_kernel(pair, after, out):
-    out[...] = pair[1]
+    out[...] = pair[0]
 
 
 def joined(later, earlier):
@@ -212,20 +216,25 @@
             send(s, j).wait()
 
 
-def image_kernel(cells, x_here, side_same, side_swapped, left, right, acc, crossing, to_left,
-                 to_right, sums, x_side, parts):
+def image_kernel(cells, x_here, side_beside, side_swapped, left, right, acc, crossing, to_first,
+                 to_second, sums, x_side, parts):
     core = place()
-    x_side[1 - core] = side_same[0]
-    x_side[core] = side_swapped[...]
+    x_side[core] = side_beside[1]
+    x_side[1 - core] = side_swapped[...]
     total = []
     for s in range(2):
         spread(parts, s, left, x_side[s], 0, QUARTER)
         image = acc[s] + folded(parts, s, right, 0, QUARTER)
         image = jnp.where(cells[s] != 0, image, 0.0).astype(BF16)
-        message = (to_left, to_right)[s]
-        message[:QUARTER] = crossing[s]
-        message[QUARTER] = image
         total.append(image)
+    odd = odd_place()
+    for is_odd in range(2):
+        @pl.when(odd == (is_odd == 1))
+        def _():
+            for s in range(2):
+                message = (to_first, to_second)[s ^ is_odd ^ 1]
+                message[:QUARTER] = crossing[s]
+                message[QUARTER] = total[s]
 
     def whole(values):
         return jnp.sum(jnp.sum(values, axis=0, keepdims=True), axis=1, keepdims=True)
@@ -243,7 +252,10 @@
     sums[...] = row
 
 
-def apart_kernel(sums, x_here, to_left, to_right, left, right, image, sums_out, parts):
+def apart_kernel(sums, x_here, to_first, to_second, left, right, image, sums_out, parts):
+    odd = odd_place()
+    first, second = to_first[QUARTER], to_second[QUARTER]
+    here = [jnp.where(odd, first, second), jnp.where(odd, second, first)]
     channels = left.shape[1]
     cross = channels - QUARTER
     ratio = sums[0:1, 2:3]
@@ -251,7 +263,7 @@
     def apart(v, x):
         return (v.astype(F32) - ratio * x.astype(F32)).astype(BF16)
 
-    inner = [apart((to_left, to_right)[s][QUARTER], x_here[s]) for s in range(2)]
+    inner = [apart(here[s], x_here[s]) for s in range(2)]
     for s in range(2):
         spread(parts, s, left, inner[s], QUARTER, cross)
         spread(parts, s, left, inner[1 - s], cross, channels)
@@ -259,11 +271,24 @@
     sums_out[...] = sums[...]
 
 
-def krylov_kernel(total_cells, cells, sums, sums_here, image, acc, x_side, from_left, from_right,
-                  left, right, table_far, env_in, krylov, env, rayleigh, parts, table,
-                  table_sem, out_sems):
-    fetch = pltpu.make_async_copy(table_far, table, table_sem.at[0])
-    fetch.start()
+def krylov_kernel(total_cells, cells, sums, sums_here, image, acc, x_side, from_first,
+                  from_second, left, right, table, env_in, krylov, env, rayleigh, parts,
+                  out_sems):
+    odd = odd_place()
+    place_of = [[table[s : s + 1, j : j + 1][0, 0] for j in range(QUARTER)] for s in range(2)]
+
+    def send(is_odd, s, j):
+        source = (from_first, from_second)[s ^ is_odd ^ 1]
+        return pltpu.make_async_copy(
+            source.at[j], env.at[0, s, place_of[s][j]], out_sems.at[s, j]
+        )
+
+    for is_odd in range(2):
+        @pl.when(odd == (is_odd == 1))
+        def _():
+            for s in range(2):
+                for j in range(QUARTER):
+                    send(is_odd, s, j).start()
     column = [jnp.sum(sums[:, i : i + 1], axis=0, keepdims=True) for i in range(2)]
     ratio = column[1] / column[0]
     apart = ratio - sums[:, 2:3]
@@ -271,26 +296,19 @@
     inverse = 1.0 / jnp.sqrt(spread_of * (1.0 / total_cells) + 1e-06)
     rayleigh[0] = ratio[0, 0]
     missing = ratio - sums_here[0:1, 2:3]
-
-    def send(s, j):
-        return pltpu.make_async_copy(
-            (from_left, from_right)[s].at[j], env.at[0, s, table[s, j]], out_sems.at[s, j]
-        )
-
-    for s in range(2):
-        arrived = (from_left, from_right)[s][QUARTER].astype(F32)
-        outer = (arrived - ratio * x_side[s].astype(F32)).astype(BF16)
+    first, second = from_first[QUARTER], from_second[QUARTER]
+    arrived = [jnp.where(odd, first, second), jnp.where(odd, second, first)]
+    for s in range(2):
+        outer = (arrived[s].astype(F32) - ratio * x_side[s].astype(F32)).astype(BF16)
         spread(parts, s, left, outer, 0, QUARTER)
-        if s == 0:
-            fetch.wait()
-            for t in range(2):
-                for j in range(QUARTER):
-                    send(t, j).start()
         whole = image[s] - missing * acc[s] + folded(parts, s, right, 0, QUARTER)
         krylov[0, s] = jnp.where(cells[s] != 0, whole * inverse, 0.0).astype(BF16)
-    for s in range(2):
-        for j in range(QUARTER):
-            send(s, j).wait()
+    for is_odd in range(2):
+        @pl.when(odd == (is_odd == 1))
+        def _():
+            for s in range(2):
+                for j in range(QUARTER):
+                    send(is_odd, s, j).wait()
 
 
 def local(state_blocks, gauge_offset, left_env, right_env, mpo_mask, charge, block_dims):
@@ -310,13 +328,18 @@
             (at(k, i), at(k + 2 * chips, i)) for k in range(segments - 2 * chips) for i in every
         ]
 
-    same = [
-        (at(2 * c + r, i), at(2 * c + r, i + 2 * r - 1))
-        for c in range(segments // 2) for r in range(2) for i in every
-        if 0 <= i + 2 * r - 1 < groups
+    beside = [
+        pair
+        for c in range(segments // 2) for i in range(groups - 1)
+        for pair in (
+            (at(2 * c + 1, i), at(2 * c, i + 1)), (at(2 * c, i + 1), at(2 * c + 1, i))
+        )
     ]
-    leftward = [(i, i - 1) for i in range(1, groups)]
-    rightward = [(i, i + 1) for i in range(groups - 1)]
+    rounds = [
+        [(i, i + 1) for i in range(first, groups - 1, 2)]
+        + [(i + 1, i) for i in range(first, groups - 1, 2)]
+        for first in range(2)
+    ]
 
     left, right = in_hbm(left_env[0]), in_hbm(right_env[0])
     whole = (2, channels) + block
@@ -380,7 +403,7 @@
         cost_estimate=cost(8, size, 2 * MIB),
     )(cells, own, got, *backs, right_sorted)
     x_swapped = lax.ppermute(x_pair, AXES, swap)
-    side_same = lax.ppermute(x_pair, AXES, same)
+    side_beside = lax.ppermute(x_pair, AXES, beside)
     acc, env, x_here, crossing = pl.pallas_call(
         own_kernel,
         out_shape=[
@@ -409,9 +432,9 @@
         out_specs=vmem(1)[0],
         compiler_params=limit(2),
         cost_estimate=cost(0, size, MIB),
-    )(side_same, acc)
+    )(side_beside, acc)
     side_swapped = lax.ppermute(relayed, AXES, swap)
-    to_left, to_right, sums, x_side = pl.pallas_call(
+    to_first, to_second, sums, x_side = pl.pallas_call(
         image_kernel,
         out_shape=[
             jax.ShapeDtypeStruct((QUARTER + 1,) + block, BF16),
@@ -424,9 +447,9 @@
         scratch_shapes=[pltpu.VMEM((2, size, QUARTER * size), BF16)],
         compiler_params=limit(10),
         cost_estimate=cost(16, size, 4 * MIB),
-    )(cells, x_here, side_same, side_swapped, left_sorted, right_sorted, acc, crossing)
-    from_right = lax.ppermute(to_left, "sec", leftward)
-    from_left = lax.ppermute(to_right, "sec", rightward)
+    )(cells, x_here, side_beside, side_swapped, left_sorted, right_sorted, acc, crossing)
+    from_first = lax.ppermute(to_first, "sec", rounds[0])
+    from_second = lax.ppermute(to_second, "sec", rounds[1])
     image, sums_here = pl.pallas_call(
         apart_kernel,
         out_shape=[
@@ -438,7 +461,7 @@
         scratch_shapes=[pltpu.VMEM((2, size, channels * size), BF16)],
         compiler_params=limit(10),
         cost_estimate=cost(48, size, 4 * MIB),
-    )(sums, x_here, to_left, to_right, left_sorted, right_sorted)
+    )(sums, x_here, to_first, to_second, left_sorted, right_sorted)
     sums = lax.all_to_all(sums_here, "sec", 0, 0)
 
     total_cells = float(groups * 2 * size * size)
@@ -449,18 +472,16 @@
             jax.ShapeDtypeStruct((1, 2, channels) + block, BF16),
             jax.ShapeDtypeStruct((1,), F32),
         ],
-        in_specs=vmem(10) + anywhere(2),
+        in_specs=vmem(11) + anywhere(1),
         out_specs=vmem(1) + anywhere(1) + smem(1),
         scratch_shapes=[
             pltpu.VMEM((2, size, QUARTER * size), BF16),
-            pltpu.SMEM((4, channels), jnp.int32),
-            pltpu.SemaphoreType.DMA((1,)),
             pltpu.SemaphoreType.DMA((2, QUARTER)),
         ],
         input_output_aliases={11: 1},
         compiler_params=limit(8),
         cost_estimate=cost(16, size, 4 * MIB),
-    )(cells, sums, sums_here, image, acc, x_side, from_left, from_right, left_sorted,
+    )(cells, sums, sums_here, image, acc, x_side, from_first, from_second, left_sorted,
       right_sorted, table, env)
     return krylov, env, rayleigh
 

time: 66.6 us -> 61.4 us (0.922)
  starting transfers between devices: 19.2 us -> 15.7 us
  Pallas kernels: 20.3 us -> 19.4 us
  blocking collectives: 24.6 us -> 23.9 us
    ppermute x3, starting transfers between devices: 8.42 us -> 4.94 us  [the longest x1 3.05 us: local(): side_beside = lax.ppermute(x_pair, AXES, beside)]
    pallas_call x1, Pallas kernels: 2.92 us -> 1.84 us  [local(): pl.pallas_call(functools.partial(krylov_kernel, total_cells), out_shape=[...]
    all_to_all x1, blocking collectives: 24.6 us -> 23.9 us  [local(): sums = lax.all_to_all(sums_here, 'sec', 0, 0)]
  transfers between devices with their start and end apart: 9 -> 9, of which waited for: 1 -> 1; matrix products, arithmetic and copies ran while one was open for 0% -> 0% of each run, Pallas kernels for 21% -> 23%
where the time goes in v3:
time: 61.4 us; the launch traced here: 61.2 us
  blocking collectives  23.9 us (39%)
  Pallas kernels  19.4 us (32%)
  starting transfers between devices  15.7 us (26%)
  waiting for transfers between devices  1.36 us (2%)
  between operations  0.78 us (1%)
    all_to_all x1, blocking collectives, local(): sums = lax.all_to_all(sums_here, 'sec', 0, 0)  23.9 us
    ppermute x3, starting transfers between devices, local(): lax.ppermute(pair, AXES, onward(chips))  6.69 us
    pallas_call x1, Pallas kernels, local(): pl.pallas_call(own_kernel, out_shape=[jax.ShapeDtypeStruct((2,) + block,...  5.39 us
    pallas_call x1, Pallas kernels, local(): pl.pallas_call(sort_kernel, out_shape=[jax.ShapeDtypeStruct(whole, BF16)]...  4.84 us
    ppermute x1, starting transfers between devices, local(): got = lax.ppermute(other, AXES, swap)  3.33 us
    ppermute x1, starting transfers between devices, local(): side_beside = lax.ppermute(x_pair, AXES, beside)  3.05 us
    pallas_call x1, Pallas kernels, local(): pl.pallas_call(apart_kernel, out_shape=[jax.ShapeDtypeStruct((2,) + block...  2.03 us
    pallas_call x1, Pallas kernels, local(): pl.pallas_call(functools.partial(krylov_kernel, total_cells), out_shape=[...  1.84 us
  transfers between devices with their start and end apart: 9, of which 1 were waited for; matrix products, arithmetic and copies ran while one was open for 0% of the time, Pallas kernels for 23%

profile of v3, /device:TPU:1, one launch (start us, length us, event | category | flops | bytes accessed | tf_op | source)
XLA Modules:
  0.0 61.2 jit_solution(6452251847091112835)
XLA Ops:
  0.6 1.2 %shard_map.95 = (bf16[2,256,256]{2,1,0:T(8,128)(2,1)S(1)}, bf16[2,256,256]{2,1,0:T(8,128)(2,1)S(1)}) custom-call(f32[2,256,256]{2,1,0:T(8,128)} %bitcast.12, bf16[2,256,256]{2,1,0:T(8,128)(2,1)} %bitcast.13), custom_call_target="tpu_custom_call" | custom-call | bytes 2097152 | tf_op jit(solution)/shard_map/pallas_call | solution.py:346
  1.8 3.3 %collective-permute-start = (bf16[2,256,256]{2,1,0:T(8,128)(2,1)S(1)}, bf16[2,256,256]{2,1,0:T(8,128)(2,1)S(1)}, u32[]{:S(2)}, u32[]{:S(2)}) collective-permute-start(bf16[2,256,256]{2,1,0:T(8,128)(2,1)S(1)} %get-tuple-element.21), channel_id=1, source_target_pairs={{0,32},{1,33},{2,34},{3,35},{4,36},{5,37},{6,38},{7,39},{8,40},{9,... | collective-permute-start | bytes 786440 | tf_op jit(solution)/shard_map/ppermute | solution.py:359
  5.1 1.6 %shard_map.94 = (bf16[2,256,256]{2,1,0:T(8,128)(2,1)S(1)}, s32[4,16]{1,0:T(4,128)S(1)}) custom-call(s32[16]{0:T(128)} %charge_far.1, s32[2,16]{1,0:T(2,128)} %mask_far.1, s32[2]{0:T(128)} %dims_far.1), custom_call_target="tpu_custom_call" | custom-call | bytes 2097152 | tf_op jit(solution)/shard_map/pallas_call | solution.py:360
  6.7 0.0 collective-permute-done.got
  6.7 0.2 shard_map.96
  6.9 2.9 %collective-permute-start.3 = (bf16[256,256]{1,0:T(8,128)(2,1)S(1)}, bf16[256,256]{1,0:T(8,128)(2,1)S(1)}, u32[]{:S(2)}, u32[]{:S(2)}) collective-permute-start(bf16[256,256]{1,0:T(8,128)(2,1)S(1)} %shard_map.96), channel_id=1, source_target_pairs={{0,192},{1,193},{2,194},{3,195},{4,196},{5,197},{6,198},{7,199},{8... | collective-permute-start | bytes 393224 | tf_op jit(solution)/shard_map/ppermute | solution.py:386
  9.8 1.3 %collective-permute-start.2 = (bf16[256,256]{1,0:T(8,128)(2,1)S(1)}, bf16[256,256]{1,0:T(8,128)(2,1)S(1)}, u32[]{:S(2)}, u32[]{:S(2)}) collective-permute-start(bf16[256,256]{1,0:T(8,128)(2,1)S(1)} %shard_map.96), channel_id=1, source_target_pairs={{0,128},{1,129},{2,130},{3,131},{4,132},{5,133},{6,134},{7,135},{8... | collective-permute-start | bytes 393224 | tf_op jit(solution)/shard_map/ppermute | solution.py:386
  11.1 2.5 %collective-permute-start.1 = (bf16[256,256]{1,0:T(8,128)(2,1)S(1)}, bf16[256,256]{1,0:T(8,128)(2,1)S(1)}, u32[]{:S(2)}, u32[]{:S(2)}) collective-permute-start(bf16[256,256]{1,0:T(8,128)(2,1)S(1)} %shard_map.96), channel_id=1, source_target_pairs={{0,64},{1,65},{2,66},{3,67},{4,68},{5,69},{6,70},{7,71},{8,72},{9,... | collective-permute-start | bytes 393224 | tf_op jit(solution)/shard_map/ppermute | solution.py:386
  13.6 4.8 %shard_map.97 = (bf16[2,16,256,256]{3,2,1,0:T(8,128)(2,1)S(1)}, bf16[2,16,256,256]{3,2,1,0:T(8,128)(2,1)S(1)}) custom-call(s32[4,16]{1,0:T(4,128)S(1)} %get-tuple-element.22.table.table_far, bf16[2,16,256,256]{3,2,1,0:T(8,128)(2,1)} %bitcast.10, bf16[2,16,256,256]{3,2,1,0:T(8,128)(2,1)} %bitcast.11), custom_call_target="tpu_custom_call" | custom-call | bytes 16777216 | tf_op jit(solution)/shard_map/pallas_call | solution.py:387
  18.5 0.0 collective-permute-done.3.three_back
  18.5 0.0 collective-permute-done.2.two_back
  18.5 0.0 collective-permute-done.1.one_back
  18.5 1.0 %shard_map.98.x_pair = bf16[2,256,256]{2,1,0:T(8,128)(2,1)S(1)} custom-call(bf16[2,256,256]{2,1,0:T(8,128)(2,1)S(1)} %get-tuple-element.19.after.cells, bf16[2,256,256]{2,1,0:T(8,128)(2,1)S(1)} %get-tuple-element.20.own, bf16[2,256,256]{2,1,0:T(8,128)(2,1)S(1)} %collective-permute-done.got, bf16[256,256]{1,0:T(8,128)(2,1)S(1)} %collective-permute-done.1.one_back, ...), custom_call_target="tpu_custom_call" | custom-call | flops 268435456 | bytes 2097152 | tf_op jit(solution)/shard_map/pallas_call | solution.py:396
  19.6 0.7 %collective-permute-start.4 = (bf16[2,256,256]{2,1,0:T(8,128)(2,1)S(1)}, bf16[2,256,256]{2,1,0:T(8,128)(2,1)S(1)}, u32[]{:S(2)}, u32[]{:S(2)}) collective-permute-start(bf16[2,256,256]{2,1,0:T(8,128)(2,1)S(1)} %shard_map.98.x_pair), channel_id=1, source_target_pairs={{0,32},{1,33},{2,34},{3,35},{4,36},{5,37},{6,38},{7,39},{8,40},{9,... | collective-permute-start | bytes 786440 | tf_op jit(solution)/shard_map/ppermute | solution.py:405
  20.2 3.0 %collective-permute-start.5 = (bf16[2,256,256]{2,1,0:T(8,128)(2,1)S(1)}, bf16[2,256,256]{2,1,0:T(8,128)(2,1)S(1)}, u32[]{:S(2)}, u32[]{:S(2)}) collective-permute-start(bf16[2,256,256]{2,1,0:T(8,128)(2,1)S(1)} %shard_map.98.x_pair), channel_id=1, source_target_pairs={{32,1},{1,32},{33,2},{2,33},{34,3},{3,34},{35,4},{4,35},{36,5},{5,... | collective-permute-start | bytes 786440 | tf_op jit(solution)/shard_map/ppermute | solution.py:406
  23.3 0.0 collective-permute-done.4.x_swapped
  23.3 5.4 %shard_map.99 = (f32[2,256,256]{2,1,0:T(8,128)S(1)}, bf16[1,2,16,256,256]{4,3,2,1,0:T(8,128)(2,1)}, bf16[2,256,256]{2,1,0:T(8,128)(2,1)S(1)}, bf16[2,4,256,256]{3,2,1,0:T(8,128)(2,1)S(1)}) custom-call(bf16[2,256,256]{2,1,0:T(8,128)(2,1)S(1)} %shard_map.98.x_pair, bf16[2,256,256]{2,1,0:T(8,128)(2,1)S(1)} %collective-permute-done.4.x_swapped, ...), custom_call_target="tpu_custom_call" | custom-call | flops 3221225472 | bytes 12582912 | tf_op jit(solution)/shard_map/pallas_call | solution.py:407
  28.7 0.0 collective-permute-done.5.pair.side_beside
  28.7 0.1 collective-permute-start.6
  28.8 1.3 %collective-permute-done.6.side_swapped = bf16[256,256]{1,0:T(8,128)(2,1)S(1)} collective-permute-done((bf16[256,256]{1,0:T(8,128)(2,1)S(1)}, bf16[256,256]{1,0:T(8,128)(2,1)S(1)}, u32[]{:S(2)}, u32[]{:S(2)}) %collective-permute-start.6) | collective-permute-done | bytes 131104 | tf_op jit(solution)/shard_map/ppermute | solution.py:436
  30.2 1.3 %shard_map.101 = (bf16[5,256,256]{2,1,0:T(8,128)(2,1)S(1)}, bf16[5,256,256]{2,1,0:T(8,128)(2,1)S(1)}, f32[32,128]{1,0:T(8,128)S(1)}, bf16[2,256,256]{2,1,0:T(8,128)(2,1)S(1)}) custom-call(bf16[2,256,256]{2,1,0:T(8,128)(2,1)S(1)} %get-tuple-element.19.after.cells, bf16[2,256,256]{2,1,0:T(8,128)(2,1)S(1)} %get-tuple-element.25.x_here, ...), custom_call_target="tpu_custom_call" | custom-call | flops 536870912 | bytes 4194304 | tf_op jit(solution)/shard_map/pallas_call | solution.py:437
  31.5 1.2 %collective-permute-start.7 = (bf16[5,256,256]{2,1,0:T(8,128)(2,1)S(1)}, bf16[5,256,256]{2,1,0:T(8,128)(2,1)S(1)}, u32[]{:S(2)}, u32[]{:S(2)}) collective-permute-start(bf16[5,256,256]{2,1,0:T(8,128)(2,1)S(1)} %get-tuple-element.29.to_first), channel_id=1, source_target_pairs={{0,1},{2,3},{4,5},{6,7},{8,9},{10,11},{12,13},{14,15},{16,17},{18,... | collective-permute-start | bytes 1966088 | tf_op jit(solution)/shard_map/ppermute | solution.py:451
  32.7 0.7 %collective-permute-start.8 = (bf16[5,256,256]{2,1,0:T(8,128)(2,1)S(1)}, bf16[5,256,256]{2,1,0:T(8,128)(2,1)S(1)}, u32[]{:S(2)}, u32[]{:S(2)}) collective-permute-start(bf16[5,256,256]{2,1,0:T(8,128)(2,1)S(1)} %get-tuple-element.30.to_second), channel_id=1, source_target_pairs={{1,2},{3,4},{5,6},{7,8},{9,10},{11,12},{13,14},{15,16},{17,18},{19... | collective-permute-start | bytes 1966088 | tf_op jit(solution)/shard_map/ppermute | solution.py:452
  33.4 2.0 %shard_map.102 = (f32[2,256,256]{2,1,0:T(8,128)S(1)}, f32[32,128]{1,0:T(8,128)S(1)}) custom-call(f32[32,128]{1,0:T(8,128)S(1)} %get-tuple-element.28.sums, bf16[2,256,256]{2,1,0:T(8,128)(2,1)S(1)} %get-tuple-element.25.x_here, bf16[5,256,256]{2,1,0:T(8,128)(2,1)S(1)} %get-tuple-element.29.to_first, bf16[5,256,256]{2,1,0:T(8,128)(2,1)S(1)} %get-tuple-element.30.to_second, ...), custom_call_target="tpu_custom_call" | custom-call | flops 1610612736 | bytes 4194304 | tf_op jit(solution)/shard_map/pallas_call | solution.py:453
  35.4 23.9 %all_to_all.11 = f32[32,1,128]{2,1,0:T(1,128)S(1)} all-to-all(f32[32,1,128]{2,1,0:T(1,128)S(1)} %bitcast.8), channel_id=1, replica_groups=mesh['seg'=8,'sec'=32] {'sec'}, dimensions={0} | all-to-all | bytes 32768 | tf_op jit(solution)/shard_map/all_to_all | solution.py:465
  59.3 0.0 collective-permute-done.7.from_first
  59.3 0.0 collective-permute-done.8.from_second
  59.3 1.8 %shard_map.103 = (bf16[1,2,256,256]{3,2,1,0:T(8,128)(2,1)}, bf16[1,2,16,256,256]{4,3,2,1,0:T(8,128)(2,1)}, f32[1]{0:T(128)}) custom-call(bf16[2,256,256]{2,1,0:T(8,128)(2,1)S(1)} %get-tuple-element.19.after.cells, f32[32,128]{1,0:T(8,128)S(1)} %bitcast.9, f32[32,128]{1,0:T(8,128)S(1)} %get-tuple-element.31.sums_here, ...), custom_call_target="tpu_custom_call", output_to_operand_aliasing={{1}: (11, {})} | custom-call | flops 536870912 | bytes 4194304 | tf_op jit(solution)/shard_map/pallas_call | solution.py:468
  (1 shorter events, 0.0 us)
Async XLA Ops:
  1.8 4.9 %collective-permute-start = (bf16[2,256,256]{2,1,0:T(8,128)(2,1)S(1)}, bf16[2,256,256]{2,1,0:T(8,128)(2,1)S(1)}, u32[]{:S(2)}, u32[]{:S(2)}) collective-permute-start(bf16[2,256,256]{2,1,0:T(8,128)(2,1)S(1)} %get-tuple-element.21), channel_id=1, source_target_pairs={{0,32},{1,33},{2,34},{3,35},{4,36},{5,37},{6,38},{7,39},{8,40},{9,... | collective-permute-start | bytes 786440 | tf_op jit(solution)/shard_map/ppermute | solution.py:359
  6.9 11.6 %collective-permute-start.3 = (bf16[256,256]{1,0:T(8,128)(2,1)S(1)}, bf16[256,256]{1,0:T(8,128)(2,1)S(1)}, u32[]{:S(2)}, u32[]{:S(2)}) collective-permute-start(bf16[256,256]{1,0:T(8,128)(2,1)S(1)} %shard_map.96), channel_id=1, source_target_pairs={{0,192},{1,193},{2,194},{3,195},{4,196},{5,197},{6,198},{7,199},{8... | collective-permute-start | bytes 393224 | tf_op jit(solution)/shard_map/ppermute | solution.py:386
  9.8 8.7 %collective-permute-start.2 = (bf16[256,256]{1,0:T(8,128)(2,1)S(1)}, bf16[256,256]{1,0:T(8,128)(2,1)S(1)}, u32[]{:S(2)}, u32[]{:S(2)}) collective-permute-start(bf16[256,256]{1,0:T(8,128)(2,1)S(1)} %shard_map.96), channel_id=1, source_target_pairs={{0,128},{1,129},{2,130},{3,131},{4,132},{5,133},{6,134},{7,135},{8... | collective-permute-start | bytes 393224 | tf_op jit(solution)/shard_map/ppermute | solution.py:386
  11.1 7.4 %collective-permute-start.1 = (bf16[256,256]{1,0:T(8,128)(2,1)S(1)}, bf16[256,256]{1,0:T(8,128)(2,1)S(1)}, u32[]{:S(2)}, u32[]{:S(2)}) collective-permute-start(bf16[256,256]{1,0:T(8,128)(2,1)S(1)} %shard_map.96), channel_id=1, source_target_pairs={{0,64},{1,65},{2,66},{3,67},{4,68},{5,69},{6,70},{7,71},{8,72},{9,... | collective-permute-start | bytes 393224 | tf_op jit(solution)/shard_map/ppermute | solution.py:386
  19.6 3.7 %collective-permute-start.4 = (bf16[2,256,256]{2,1,0:T(8,128)(2,1)S(1)}, bf16[2,256,256]{2,1,0:T(8,128)(2,1)S(1)}, u32[]{:S(2)}, u32[]{:S(2)}) collective-permute-start(bf16[2,256,256]{2,1,0:T(8,128)(2,1)S(1)} %shard_map.98.x_pair), channel_id=1, source_target_pairs={{0,32},{1,33},{2,34},{3,35},{4,36},{5,37},{6,38},{7,39},{8,40},{9,... | collective-permute-start | bytes 786440 | tf_op jit(solution)/shard_map/ppermute | solution.py:405
  20.2 8.5 %collective-permute-start.5 = (bf16[2,256,256]{2,1,0:T(8,128)(2,1)S(1)}, bf16[2,256,256]{2,1,0:T(8,128)(2,1)S(1)}, u32[]{:S(2)}, u32[]{:S(2)}) collective-permute-start(bf16[2,256,256]{2,1,0:T(8,128)(2,1)S(1)} %shard_map.98.x_pair), channel_id=1, source_target_pairs={{32,1},{1,32},{33,2},{2,33},{34,3},{3,34},{35,4},{4,35},{36,5},{5,... | collective-permute-start | bytes 786440 | tf_op jit(solution)/shard_map/ppermute | solution.py:406
  28.7 1.4 %collective-permute-start.6 = (bf16[256,256]{1,0:T(8,128)(2,1)S(1)}, bf16[256,256]{1,0:T(8,128)(2,1)S(1)}, u32[]{:S(2)}, u32[]{:S(2)}) collective-permute-start(bf16[256,256]{1,0:T(8,128)(2,1)S(1)} %shard_map.100), channel_id=1, source_target_pairs={{0,32},{1,33},{2,34},{3,35},{4,36},{5,37},{6,38},{7,39},{8,40},{9,... | collective-permute-start | bytes 393224 | tf_op jit(solution)/shard_map/ppermute | solution.py:436
  31.5 27.8 %collective-permute-start.7 = (bf16[5,256,256]{2,1,0:T(8,128)(2,1)S(1)}, bf16[5,256,256]{2,1,0:T(8,128)(2,1)S(1)}, u32[]{:S(2)}, u32[]{:S(2)}) collective-permute-start(bf16[5,256,256]{2,1,0:T(8,128)(2,1)S(1)} %get-tuple-element.29.to_first), channel_id=1, source_target_pairs={{0,1},{2,3},{4,5},{6,7},{8,9},{10,11},{12,13},{14,15},{16,17},{18,... | collective-permute-start | bytes 1966088 | tf_op jit(solution)/shard_map/ppermute | solution.py:451
  32.7 26.6 %collective-permute-start.8 = (bf16[5,256,256]{2,1,0:T(8,128)(2,1)S(1)}, bf16[5,256,256]{2,1,0:T(8,128)(2,1)S(1)}, u32[]{:S(2)}, u32[]{:S(2)}) collective-permute-start(bf16[5,256,256]{2,1,0:T(8,128)(2,1)S(1)} %get-tuple-element.30.to_second), channel_id=1, source_target_pairs={{1,2},{3,4},{5,6},{7,8},{9,10},{11,12},{13,14},{15,16},{17,18},{19... | collective-permute-start | bytes 1966088 | tf_op jit(solution)/shard_map/ppermute | solution.py:452

commit v4 on v3

--- a/solution.py
+++ b/solution.py
@@ -179,8 +179,8 @@
     return dot(parts[s, :, first * size : last * size], rows)
 
 
-def own_kernel(x_pair, x_swapped, left, right, table_far, acc, env, x_here, crossing, parts,
-               blocks, table, table_sem, out_sems):
+def own_kernel(x_pair, x_swapped, left, table_far, env, x_here, crossing, parts, blocks, table,
+               table_sem, out_sems):
     core = place()
     channels, size = left.shape[1], left.shape[2]
     cross = channels - QUARTER
@@ -209,11 +209,20 @@
         for j in range(cross):
             send(s, j).start()
     for s in range(2):
-        spread(parts, s, left, x_here[1 - s], cross, channels)
-        acc[s] = folded(parts, s, right, QUARTER, channels)
-    for s in range(2):
         for j in range(cross):
             send(s, j).wait()
+
+
+def inner_kernel(x_here, left, right, parts, after, acc, side_parts):
+    channels, size = left.shape[1], left.shape[2]
+    cross = channels - QUARTER
+    for s in range(2):
+        rows = left[s, cross:channels].reshape(QUARTER * size, size)
+        result = dot(rows, x_here[1 - s]).astype(BF16)
+        for j in range(QUARTER):
+            side_parts[s, :, j * size : (j + 1) * size] = result[j * size : (j + 1) * size]
+        rows = right[s, cross:channels].reshape(QUARTER * size, size)
+        acc[s] = folded(parts, s, right, QUARTER, cross) + dot(side_parts[s], rows)
 
 
 def image_kernel(cells, x_here, side_beside, side_swapped, left, right, acc, crossing, to_first,
@@ -404,26 +413,25 @@
     )(cells, own, got, *backs, right_sorted)
     x_swapped = lax.ppermute(x_pair, AXES, swap)
     side_beside = lax.ppermute(x_pair, AXES, beside)
-    acc, env, x_here, crossing = pl.pallas_call(
+    env, x_here, crossing, parts = pl.pallas_call(
         own_kernel,
         out_shape=[
-            jax.ShapeDtypeStruct((2,) + block, F32),
             pltpu.HBM((1, 2, channels) + block, BF16),
             jax.ShapeDtypeStruct((2,) + block, BF16),
             jax.ShapeDtypeStruct((2, QUARTER) + block, BF16),
-        ],
-        in_specs=vmem(4) + anywhere(1),
-        out_specs=vmem(1) + anywhere(1) + vmem(2),
+            jax.ShapeDtypeStruct((2, size, channels * size), BF16),
+        ],
+        in_specs=vmem(3) + anywhere(1),
+        out_specs=anywhere(1) + vmem(3),
         scratch_shapes=[
-            pltpu.VMEM((2, size, channels * size), BF16),
             pltpu.VMEM((2, channels - QUARTER) + block, BF16),
             pltpu.SMEM((4, channels), jnp.int32),
             pltpu.SemaphoreType.DMA((1,)),
             pltpu.SemaphoreType.DMA((2, channels - QUARTER)),
         ],
         compiler_params=limit(12),
-        cost_estimate=cost(96, size, 12 * MIB),
-    )(x_pair, x_swapped, left_sorted, right_sorted, table)
+        cost_estimate=cost(72, size, 12 * MIB),
+    )(x_pair, x_swapped, left_sorted, table)
 
     relayed = pl.pallas_call(
         relay_kernel,
@@ -432,8 +440,17 @@
         out_specs=vmem(1)[0],
         compiler_params=limit(2),
         cost_estimate=cost(0, size, MIB),
-    )(side_beside, acc)
+    )(side_beside, x_here)
     side_swapped = lax.ppermute(relayed, AXES, swap)
+    acc = pl.pallas_call(
+        inner_kernel,
+        out_shape=jax.ShapeDtypeStruct((2,) + block, F32),
+        in_specs=vmem(4) + anywhere(1),
+        out_specs=vmem(1)[0],
+        scratch_shapes=[pltpu.VMEM((2, size, QUARTER * size), BF16)],
+        compiler_params=limit(10),
+        cost_estimate=cost(32, size, 4 * MIB),
+    )(x_here, left_sorted, right_sorted, parts, relayed)
     to_first, to_second, sums, x_side = pl.pallas_call(
         image_kernel,
         out_shape=[

time: 61.4 us -> 61.3 us (level)
  waiting for transfers between devices: 1.36 us -> 0.69 us
    ppermute x1, waiting for transfers between devices: 1.33 us -> 0.08 us  [local(): side_swapped = lax.ppermute(relayed, AXES, swap)]
    all_to_all x1, blocking collectives: 23.9 us -> 24.5 us  [local(): sums = lax.all_to_all(sums_here, 'sec', 0, 0)]
    pallas_call x1 -> x2, Pallas kernels: 5.39 us -> 5.26 us  [the longest x1 4.02 us: local(): pl.pallas_call(own_kernel, out_shape=[pltpu.HBM((1, 2, channels) + block,...]
  transfers between devices with their start and end apart: 9 -> 9, of which waited for: 1 -> 2; matrix products, arithmetic and copies ran while one was open for 0% -> 0% of each run, Pallas kernels for 23% -> 22%
where the time goes in v4:
time: 61.3 us; the launch traced here: 61 us
  blocking collectives  24.5 us (40%)
  Pallas kernels  19.3 us (31%)
  starting transfers between devices  15.8 us (26%)
  between operations  0.78 us (1%)
  waiting for transfers between devices  0.69 us (1%)
    all_to_all x1, blocking collectives, local(): sums = lax.all_to_all(sums_here, 'sec', 0, 0)  24.5 us
    ppermute x3, starting transfers between devices, local(): lax.ppermute(pair, AXES, onward(chips))  6.69 us
    pallas_call x1, Pallas kernels, local(): pl.pallas_call(sort_kernel, out_shape=[jax.ShapeDtypeStruct(whole, BF16)]...  4.81 us
    pallas_call x1, Pallas kernels, local(): pl.pallas_call(own_kernel, out_shape=[pltpu.HBM((1, 2, channels) + block,...  4.02 us
    ppermute x1, starting transfers between devices, local(): got = lax.ppermute(other, AXES, swap)  3.33 us
    ppermute x1, starting transfers between devices, local(): side_beside = lax.ppermute(x_pair, AXES, beside)  3.05 us
    pallas_call x1, Pallas kernels, local(): pl.pallas_call(apart_kernel, out_shape=[jax.ShapeDtypeStruct((2,) + block...  2.03 us
    pallas_call x1, Pallas kernels, local(): pl.pallas_call(functools.partial(krylov_kernel, total_cells), out_shape=[...  1.85 us
  transfers between devices with their start and end apart: 9, of which 2 were waited for; matrix products, arithmetic and copies ran while one was open for 0% of the time, Pallas kernels for 22%

profile of v4, /device:TPU:1, one launch (start us, length us, event | category | flops | bytes accessed | tf_op | source)
XLA Modules:
  0.0 61.0 jit_solution(10411078144150018774)
XLA Ops:
  0.6 1.2 %shard_map.95 = (bf16[2,256,256]{2,1,0:T(8,128)(2,1)S(1)}, bf16[2,256,256]{2,1,0:T(8,128)(2,1)S(1)}) custom-call(f32[2,256,256]{2,1,0:T(8,128)} %bitcast.12, bf16[2,256,256]{2,1,0:T(8,128)(2,1)} %bitcast.13), custom_call_target="tpu_custom_call" | custom-call | bytes 2097152 | tf_op jit(solution)/shard_map/pallas_call | solution.py:355
  1.8 3.3 %collective-permute-start = (bf16[2,256,256]{2,1,0:T(8,128)(2,1)S(1)}, bf16[2,256,256]{2,1,0:T(8,128)(2,1)S(1)}, u32[]{:S(2)}, u32[]{:S(2)}) collective-permute-start(bf16[2,256,256]{2,1,0:T(8,128)(2,1)S(1)} %get-tuple-element.21), channel_id=1, source_target_pairs={{0,32},{1,33},{2,34},{3,35},{4,36},{5,37},{6,38},{7,39},{8,40},{9,... | collective-permute-start | bytes 786440 | tf_op jit(solution)/shard_map/ppermute | solution.py:368
  5.1 1.6 %shard_map.94 = (bf16[2,256,256]{2,1,0:T(8,128)(2,1)S(1)}, s32[4,16]{1,0:T(4,128)S(1)}) custom-call(s32[16]{0:T(128)} %charge_far.1, s32[2,16]{1,0:T(2,128)} %mask_far.1, s32[2]{0:T(128)} %dims_far.1), custom_call_target="tpu_custom_call" | custom-call | bytes 2097152 | tf_op jit(solution)/shard_map/pallas_call | solution.py:369
  6.7 0.0 collective-permute-done.got
  6.7 0.2 shard_map.96
  6.9 2.9 %collective-permute-start.3 = (bf16[256,256]{1,0:T(8,128)(2,1)S(1)}, bf16[256,256]{1,0:T(8,128)(2,1)S(1)}, u32[]{:S(2)}, u32[]{:S(2)}) collective-permute-start(bf16[256,256]{1,0:T(8,128)(2,1)S(1)} %shard_map.96), channel_id=1, source_target_pairs={{0,192},{1,193},{2,194},{3,195},{4,196},{5,197},{6,198},{7,199},{8... | collective-permute-start | bytes 393224 | tf_op jit(solution)/shard_map/ppermute | solution.py:395
  9.8 1.3 %collective-permute-start.2 = (bf16[256,256]{1,0:T(8,128)(2,1)S(1)}, bf16[256,256]{1,0:T(8,128)(2,1)S(1)}, u32[]{:S(2)}, u32[]{:S(2)}) collective-permute-start(bf16[256,256]{1,0:T(8,128)(2,1)S(1)} %shard_map.96), channel_id=1, source_target_pairs={{0,128},{1,129},{2,130},{3,131},{4,132},{5,133},{6,134},{7,135},{8... | collective-permute-start | bytes 393224 | tf_op jit(solution)/shard_map/ppermute | solution.py:395
  11.1 2.5 %collective-permute-start.1 = (bf16[256,256]{1,0:T(8,128)(2,1)S(1)}, bf16[256,256]{1,0:T(8,128)(2,1)S(1)}, u32[]{:S(2)}, u32[]{:S(2)}) collective-permute-start(bf16[256,256]{1,0:T(8,128)(2,1)S(1)} %shard_map.96), channel_id=1, source_target_pairs={{0,64},{1,65},{2,66},{3,67},{4,68},{5,69},{6,70},{7,71},{8,72},{9,... | collective-permute-start | bytes 393224 | tf_op jit(solution)/shard_map/ppermute | solution.py:395
  13.6 4.8 %shard_map.97 = (bf16[2,16,256,256]{3,2,1,0:T(8,128)(2,1)S(1)}, bf16[2,16,256,256]{3,2,1,0:T(8,128)(2,1)S(1)}) custom-call(s32[4,16]{1,0:T(4,128)S(1)} %get-tuple-element.22.table.table_far, bf16[2,16,256,256]{3,2,1,0:T(8,128)(2,1)} %bitcast.10, bf16[2,16,256,256]{3,2,1,0:T(8,128)(2,1)} %bitcast.11), custom_call_target="tpu_custom_call" | custom-call | bytes 16777216 | tf_op jit(solution)/shard_map/pallas_call | solution.py:396
  18.4 0.0 collective-permute-done.3.three_back
  18.5 0.0 collective-permute-done.2.two_back
  18.5 0.0 collective-permute-done.1.one_back
  18.5 1.0 %shard_map.98.x_pair = bf16[2,256,256]{2,1,0:T(8,128)(2,1)S(1)} custom-call(bf16[2,256,256]{2,1,0:T(8,128)(2,1)S(1)} %get-tuple-element.19.after.cells, bf16[2,256,256]{2,1,0:T(8,128)(2,1)S(1)} %get-tuple-element.20.own, bf16[2,256,256]{2,1,0:T(8,128)(2,1)S(1)} %collective-permute-done.got, bf16[256,256]{1,0:T(8,128)(2,1)S(1)} %collective-permute-done.1.one_back, ...), custom_call_target="tpu_custom_call" | custom-call | flops 268435456 | bytes 2097152 | tf_op jit(solution)/shard_map/pallas_call | solution.py:405
  19.5 0.7 %collective-permute-start.4 = (bf16[2,256,256]{2,1,0:T(8,128)(2,1)S(1)}, bf16[2,256,256]{2,1,0:T(8,128)(2,1)S(1)}, u32[]{:S(2)}, u32[]{:S(2)}) collective-permute-start(bf16[2,256,256]{2,1,0:T(8,128)(2,1)S(1)} %shard_map.98.x_pair), channel_id=1, source_target_pairs={{0,32},{1,33},{2,34},{3,35},{4,36},{5,37},{6,38},{7,39},{8,40},{9,... | collective-permute-start | bytes 786440 | tf_op jit(solution)/shard_map/ppermute | solution.py:414
  20.2 3.0 %collective-permute-start.5 = (bf16[2,256,256]{2,1,0:T(8,128)(2,1)S(1)}, bf16[2,256,256]{2,1,0:T(8,128)(2,1)S(1)}, u32[]{:S(2)}, u32[]{:S(2)}) collective-permute-start(bf16[2,256,256]{2,1,0:T(8,128)(2,1)S(1)} %shard_map.98.x_pair), channel_id=1, source_target_pairs={{32,1},{1,32},{33,2},{2,33},{34,3},{3,34},{35,4},{4,35},{36,5},{5,... | collective-permute-start | bytes 786440 | tf_op jit(solution)/shard_map/ppermute | solution.py:415
  23.3 0.0 collective-permute-done.4.x_swapped
  23.3 4.0 %shard_map.99 = (bf16[1,2,16,256,256]{4,3,2,1,0:T(8,128)(2,1)}, bf16[2,256,256]{2,1,0:T(8,128)(2,1)S(1)}, bf16[2,4,256,256]{3,2,1,0:T(8,128)(2,1)S(1)}, bf16[2,256,4096]{2,1,0:T(8,128)(2,1)S(1)}) custom-call(bf16[2,256,256]{2,1,0:T(8,128)(2,1)S(1)} %shard_map.98.x_pair, bf16[2,256,256]{2,1,0:T(8,128)(2,1)S(1)} %collective-permute-done.4.x_swapped, ...), custom_call_target="tpu_custom_call" | custom-call | flops 2415919104 | bytes 12582912 | tf_op jit(solution)/shard_map/pallas_call | solution.py:416
  27.3 0.6 collective-permute-done.5.pair.side_beside
  27.9 0.1 collective-permute-start.6
  28.0 1.2 %shard_map.101.acc = f32[2,256,256]{2,1,0:T(8,128)S(1)} custom-call(bf16[2,256,256]{2,1,0:T(8,128)(2,1)S(1)} %get-tuple-element.25.after.x_here, bf16[2,16,256,256]{3,2,1,0:T(8,128)(2,1)S(1)} %get-tuple-element.24.left, bf16[2,16,256,256]{3,2,1,0:T(8,128)(2,1)S(1)} %get-tuple-element.23.refs_0_.right, bf16[2,256,4096]{2,1,0:T(8,128)(2,1)S(1)} %get-tuple-element.26.parts, ...), custom_call_target="tpu_custom_call" | custom-call | flops 1073741824 | bytes 4194304 | tf_op jit(solution)/shard_map/pallas_call | solution.py:445
  29.2 0.1 collective-permute-done.6.side_swapped
  29.3 1.3 %shard_map.102 = (bf16[5,256,256]{2,1,0:T(8,128)(2,1)S(1)}, bf16[5,256,256]{2,1,0:T(8,128)(2,1)S(1)}, f32[32,128]{1,0:T(8,128)S(1)}, bf16[2,256,256]{2,1,0:T(8,128)(2,1)S(1)}) custom-call(bf16[2,256,256]{2,1,0:T(8,128)(2,1)S(1)} %get-tuple-element.19.after.cells, bf16[2,256,256]{2,1,0:T(8,128)(2,1)S(1)} %get-tuple-element.25.after.x_here, ...), custom_call_target="tpu_custom_call" | custom-call | flops 536870912 | bytes 4194304 | tf_op jit(solution)/shard_map/pallas_call | solution.py:454
  30.7 1.3 %collective-permute-start.7 = (bf16[5,256,256]{2,1,0:T(8,128)(2,1)S(1)}, bf16[5,256,256]{2,1,0:T(8,128)(2,1)S(1)}, u32[]{:S(2)}, u32[]{:S(2)}) collective-permute-start(bf16[5,256,256]{2,1,0:T(8,128)(2,1)S(1)} %get-tuple-element.29.to_first), channel_id=1, source_target_pairs={{0,1},{2,3},{4,5},{6,7},{8,9},{10,11},{12,13},{14,15},{16,17},{18,... | collective-permute-start | bytes 1966088 | tf_op jit(solution)/shard_map/ppermute | solution.py:468
  31.9 0.7 %collective-permute-start.8 = (bf16[5,256,256]{2,1,0:T(8,128)(2,1)S(1)}, bf16[5,256,256]{2,1,0:T(8,128)(2,1)S(1)}, u32[]{:S(2)}, u32[]{:S(2)}) collective-permute-start(bf16[5,256,256]{2,1,0:T(8,128)(2,1)S(1)} %get-tuple-element.30.to_second), channel_id=1, source_target_pairs={{1,2},{3,4},{5,6},{7,8},{9,10},{11,12},{13,14},{15,16},{17,18},{19... | collective-permute-start | bytes 1966088 | tf_op jit(solution)/shard_map/ppermute | solution.py:469
  32.6 2.0 %shard_map.103 = (f32[2,256,256]{2,1,0:T(8,128)S(1)}, f32[32,128]{1,0:T(8,128)S(1)}) custom-call(f32[32,128]{1,0:T(8,128)S(1)} %get-tuple-element.28.sums, bf16[2,256,256]{2,1,0:T(8,128)(2,1)S(1)} %get-tuple-element.25.after.x_here, bf16[5,256,256]{2,1,0:T(8,128)(2,1)S(1)} %get-tuple-element.29.to_first, ...), custom_call_target="tpu_custom_call" | custom-call | flops 1610612736 | bytes 4194304 | tf_op jit(solution)/shard_map/pallas_call | solution.py:470
  34.6 24.5 %all_to_all.11 = f32[32,1,128]{2,1,0:T(1,128)S(1)} all-to-all(f32[32,1,128]{2,1,0:T(1,128)S(1)} %bitcast.8), channel_id=1, replica_groups=mesh['seg'=8,'sec'=32] {'sec'}, dimensions={0} | all-to-all | bytes 32768 | tf_op jit(solution)/shard_map/all_to_all | solution.py:482
  59.2 0.0 collective-permute-done.7.from_first
  59.2 0.0 collective-permute-done.8.from_second
  59.2 1.8 %shard_map.104 = (bf16[1,2,256,256]{3,2,1,0:T(8,128)(2,1)}, bf16[1,2,16,256,256]{4,3,2,1,0:T(8,128)(2,1)}, f32[1]{0:T(128)}) custom-call(bf16[2,256,256]{2,1,0:T(8,128)(2,1)S(1)} %get-tuple-element.19.after.cells, f32[32,128]{1,0:T(8,128)S(1)} %bitcast.9, f32[32,128]{1,0:T(8,128)S(1)} %get-tuple-element.31.sums_here, ...), custom_call_target="tpu_custom_call", output_to_operand_aliasing={{1}: (11, {})} | custom-call | flops 536870912 | bytes 4194304 | tf_op jit(solution)/shard_map/pallas_call | solution.py:485
  (1 shorter events, 0.0 us)
Async XLA Ops:
  1.8 4.9 %collective-permute-start = (bf16[2,256,256]{2,1,0:T(8,128)(2,1)S(1)}, bf16[2,256,256]{2,1,0:T(8,128)(2,1)S(1)}, u32[]{:S(2)}, u32[]{:S(2)}) collective-permute-start(bf16[2,256,256]{2,1,0:T(8,128)(2,1)S(1)} %get-tuple-element.21), channel_id=1, source_target_pairs={{0,32},{1,33},{2,34},{3,35},{4,36},{5,37},{6,38},{7,39},{8,40},{9,... | collective-permute-start | bytes 786440 | tf_op jit(solution)/shard_map/ppermute | solution.py:368
  6.9 11.5 %collective-permute-start.3 = (bf16[256,256]{1,0:T(8,128)(2,1)S(1)}, bf16[256,256]{1,0:T(8,128)(2,1)S(1)}, u32[]{:S(2)}, u32[]{:S(2)}) collective-permute-start(bf16[256,256]{1,0:T(8,128)(2,1)S(1)} %shard_map.96), channel_id=1, source_target_pairs={{0,192},{1,193},{2,194},{3,195},{4,196},{5,197},{6,198},{7,199},{8... | collective-permute-start | bytes 393224 | tf_op jit(solution)/shard_map/ppermute | solution.py:395
  9.8 8.6 %collective-permute-start.2 = (bf16[256,256]{1,0:T(8,128)(2,1)S(1)}, bf16[256,256]{1,0:T(8,128)(2,1)S(1)}, u32[]{:S(2)}, u32[]{:S(2)}) collective-permute-start(bf16[256,256]{1,0:T(8,128)(2,1)S(1)} %shard_map.96), channel_id=1, source_target_pairs={{0,128},{1,129},{2,130},{3,131},{4,132},{5,133},{6,134},{7,135},{8... | collective-permute-start | bytes 393224 | tf_op jit(solution)/shard_map/ppermute | solution.py:395
  11.1 7.3 %collective-permute-start.1 = (bf16[256,256]{1,0:T(8,128)(2,1)S(1)}, bf16[256,256]{1,0:T(8,128)(2,1)S(1)}, u32[]{:S(2)}, u32[]{:S(2)}) collective-permute-start(bf16[256,256]{1,0:T(8,128)(2,1)S(1)} %shard_map.96), channel_id=1, source_target_pairs={{0,64},{1,65},{2,66},{3,67},{4,68},{5,69},{6,70},{7,71},{8,72},{9,... | collective-permute-start | bytes 393224 | tf_op jit(solution)/shard_map/ppermute | solution.py:395
  19.5 3.7 %collective-permute-start.4 = (bf16[2,256,256]{2,1,0:T(8,128)(2,1)S(1)}, bf16[2,256,256]{2,1,0:T(8,128)(2,1)S(1)}, u32[]{:S(2)}, u32[]{:S(2)}) collective-permute-start(bf16[2,256,256]{2,1,0:T(8,128)(2,1)S(1)} %shard_map.98.x_pair), channel_id=1, source_target_pairs={{0,32},{1,33},{2,34},{3,35},{4,36},{5,37},{6,38},{7,39},{8,40},{9,... | collective-permute-start | bytes 786440 | tf_op jit(solution)/shard_map/ppermute | solution.py:414
  20.2 7.7 %collective-permute-start.5 = (bf16[2,256,256]{2,1,0:T(8,128)(2,1)S(1)}, bf16[2,256,256]{2,1,0:T(8,128)(2,1)S(1)}, u32[]{:S(2)}, u32[]{:S(2)}) collective-permute-start(bf16[2,256,256]{2,1,0:T(8,128)(2,1)S(1)} %shard_map.98.x_pair), channel_id=1, source_target_pairs={{32,1},{1,32},{33,2},{2,33},{34,3},{3,34},{35,4},{4,35},{36,5},{5,... | collective-permute-start | bytes 786440 | tf_op jit(solution)/shard_map/ppermute | solution.py:415
  27.9 1.4 %collective-permute-start.6 = (bf16[256,256]{1,0:T(8,128)(2,1)S(1)}, bf16[256,256]{1,0:T(8,128)(2,1)S(1)}, u32[]{:S(2)}, u32[]{:S(2)}) collective-permute-start(bf16[256,256]{1,0:T(8,128)(2,1)S(1)} %shard_map.100.after), channel_id=1, source_target_pairs={{0,32},{1,33},{2,34},{3,35},{4,36},{5,37},{6,38},{7,39},{8,40},{9,... | collective-permute-start | bytes 393224 | tf_op jit(solution)/shard_map/ppermute | solution.py:444
  30.7 28.5 %collective-permute-start.7 = (bf16[5,256,256]{2,1,0:T(8,128)(2,1)S(1)}, bf16[5,256,256]{2,1,0:T(8,128)(2,1)S(1)}, u32[]{:S(2)}, u32[]{:S(2)}) collective-permute-start(bf16[5,256,256]{2,1,0:T(8,128)(2,1)S(1)} %get-tuple-element.29.to_first), channel_id=1, source_target_pairs={{0,1},{2,3},{4,5},{6,7},{8,9},{10,11},{12,13},{14,15},{16,17},{18,... | collective-permute-start | bytes 1966088 | tf_op jit(solution)/shard_map/ppermute | solution.py:468
  31.9 27.3 %collective-permute-start.8 = (bf16[5,256,256]{2,1,0:T(8,128)(2,1)S(1)}, bf16[5,256,256]{2,1,0:T(8,128)(2,1)S(1)}, u32[]{:S(2)}, u32[]{:S(2)}) collective-permute-start(bf16[5,256,256]{2,1,0:T(8,128)(2,1)S(1)} %get-tuple-element.30.to_second), channel_id=1, source_target_pairs={{1,2},{3,4},{5,6},{7,8},{9,10},{11,12},{13,14},{15,16},{17,18},{19... | collective-permute-start | bytes 1966088 | tf_op jit(solution)/shard_map/ppermute | solution.py:469
